TPU v7x, 256 devices: a whole 4x4x8 slice. The times are simulated.
256 devices in a mesh: row: 8 (over y, core), col: 32 (over z, x).
Axes of the slice: x: 4, y: 4, z: 8, core: 2. Of those that a mesh axis runs over, the one named last changes fastest.
Arguments:
- momentum: float32 [8192, 14336], P('row', 'col'), may hold values from -12 to 12
- gradient: float32 [8192, 14336], P('row', 'col'), may hold values from -6 to 6
- right_factor: float32 [14336, 256], P('col'), may hold values from -0.046875 to 0.046875
Outputs:
- momentum_next: float32 [8192, 14336], P('row', 'col')
- update: float32 [8192, 14336], P('row', 'col')
All inputs are finite; a program needn't handle non-finite values.
Results may differ from a plain program's by a relative error of at most 0.002.
Values sent between devices are 32-bit elements; how exact they have to be, the bound alone decides.
No kernel may reach another device: no remote copies, remote signals or barrier semaphores. Data moves between devices by JAX's collectives and lax.ppermute only.
A program may use at most 64 MiB of HBM per device.

v0:
```python
import jax
import jax.numpy as jnp
from jax import lax
from jax.sharding import PartitionSpec as P

D = 8192
FF = 14336
RANK = 256
ITERS = 2


MU = 0.95


def solve_left(left, gram):
    lower = jnp.linalg.cholesky(gram)
    return lax.linalg.triangular_solve(lower, left, left_side=False, lower=True, transpose_a=True)


def gram_of(left):
    return lax.dot_general(left, left, (((0,), (0,)), ((), ())), precision=lax.Precision.HIGHEST)


def on_device(momentum, gradient, right_factor):
    buffer = momentum + gradient
    right = right_factor
    left = None
    carried = None
    for step in range(ITERS):
        partial_value = jnp.dot(buffer, right, precision=lax.Precision.HIGHEST)
        left = lax.psum(partial_value, "col")
        gram = lax.psum(gram_of(left), "row")
        left = solve_left(left, gram)
        partial_value = lax.dot_general(
            buffer, left, (((0,), (0,)), ((), ())), precision=lax.Precision.HIGHEST
        )
        carried = lax.psum(partial_value, "row")
        squares = lax.psum(jnp.sum(carried * carried, axis=0), "col")
        right = carried / jnp.sqrt(squares + 1e-06)
    feedback = lax.dot_general(
        left, carried, (((1,), (1,)), ((), ())), precision=lax.Precision.HIGHEST
    )
    momentum_next = buffer - (1.0 - MU) * feedback
    factor = jnp.float32((D * FF / RANK) ** 0.5)
    update = factor * lax.dot_general(
        left, right, (((1,), (1,)), ((), ())), precision=lax.Precision.HIGHEST
    )
    return (momentum_next, update)


def solution(mesh):
    return jax.shard_map(
        on_device,
        mesh=mesh,
        in_specs=(P("row", "col"), P("row", "col"), P("col", None)),
        out_specs=(P("row", "col"), P("row", "col")),
        check_vma=False,
    )
```

profile of v0, /device:TPU:8, one launch (start us, length us, event | category | flops | bytes accessed | tf_op | source)
XLA Modules:
  0.0 889.8 jit_solution(10848033784972004305)
XLA Ops:
  7.2 2.5 add.42
  9.8 4.4 fusion.36
  14.3 152.4 %all-reduce.8.cloned.1.call-done = f32[1024,256]{1,0:T(8,128)} async-done(((f32[1024,256]{1,0:T(8,128)}), f32[1024,256]{1,0:T(8,128)}) %all-reduce.8.cloned.1.call-update) | async-done | bytes 1048592 | tf_op jit(solution)/shard_map/psum | solution.py:31
  166.7 4.1 fusion.37
  171.3 59.8 %all-reduce.10.cloned.1.call-done = f32[256,256]{0,1:T(8,128)} async-done(((f32[256,256]{0,1:T(8,128)}), f32[256,256]{0,1:T(8,128)}) %all-reduce.10.cloned.1.call-update) | async-done | bytes 262160 | tf_op jit(solution)/shard_map/psum | solution.py:32
  231.1 1.8 copy.6
  232.9 1.2 fusion.13
  234.1 0.7 copy-done.3
  234.8 11.7 %cholesky.130 = f32[128,128]{1,0:T(8,128)S(1)} custom-call(f32[128,128]{1,0:T(8,128)S(1)} %cholesky.194), custom_call_target="Cholesky" | custom-call | tf_op jit(solution)/shard_map/jit(cholesky)/cholesky | solution.py:16
  246.5 9.8 %custom-call.13 = f32[1,128,128]{1,2,0:T(8,128)S(1)} custom-call(f32[1,128,128]{2,1,0:T(8,128)S(1)} %get-tuple-element.47), custom_call_target="InvertDiagBlocksLowerTriangular" | custom-call | tf_op jit(solution)/shard_map/jit(cholesky)/cholesky | solution.py:16
  256.3 0.7 cholesky.155
  257.1 1.7 constant_dynamic-update-slice_fusion.3
  258.7 1.1 convolution_subtract_fusion.3
  259.8 11.7 %cholesky.147 = f32[128,128]{1,0:T(8,128)S(1)} custom-call(f32[128,128]{1,0:T(8,128)S(1)} %convolution_subtract_fusion.3), custom_call_target="Cholesky" | custom-call | tf_op jit(solution)/shard_map/jit(cholesky)/cholesky | solution.py:16
  271.5 0.6 fusion.29
  272.2 0.7 compare_reduce_fusion.2
  274.2 1.7 select_select_fusion.1
  276.0 6.0 while.4
  276.8 2.3 bitcast_dynamic-update-slice_fusion.4
  279.8 2.3 bitcast_dynamic-update-slice_fusion.4
  282.1 0.6 copy-done.4
  282.7 20.5 %custom-call.14 = f32[2,128,128]{1,2,0:T(8,128)S(1)} custom-call(f32[2,128,128]{2,1,0:T(8,128)} %copy-done.4), custom_call_target="InvertDiagBlocksLowerTriangular" | custom-call | tf_op jit(solution)/shard_map/triangular_solve/custom-call.0 | solution.py:17
  303.9 1.8 convolution_subtract_fusion.1
  306.3 2.4 fusion
  308.8 64.8 %all-reduce.12.cloned.1.call-done = f32[448,256]{1,0:T(8,128)} async-done(((f32[448,256]{1,0:T(8,128)}), f32[448,256]{1,0:T(8,128)}) %all-reduce.12.cloned.1.call-update) | async-done | bytes 458768 | tf_op jit(solution)/shard_map/psum | solution.py:37
  373.7 1.1 multiply_reduce_fusion.1
  374.8 75.0 %psum.59 = f32[256]{0:T(256)S(1)} all-reduce(f32[256]{0:T(256)S(1)} %multiply_reduce_fusion.1), channel_id=1, replica_groups=mesh['row'=8,'col'=32] {'col'}, use_global_device_ids=true, to_apply=%region_8.11 | all-reduce | flops 256 | bytes 2048 | tf_op jit(solution)/shard_map/psum | solution.py:38
  449.8 5.4 fusion.10
  455.3 145.3 %all-reduce.14.cloned.1.call-done = f32[1024,256]{1,0:T(8,128)} async-done(((f32[1024,256]{1,0:T(8,128)}), f32[1024,256]{1,0:T(8,128)}) %all-reduce.14.cloned.1.call-update) | async-done | bytes 1048592 | tf_op jit(solution)/shard_map/psum | solution.py:31
  600.6 4.1 fusion.38
  605.0 60.1 %all-reduce.16.cloned.1.call-done = f32[256,256]{0,1:T(8,128)} async-done(((f32[256,256]{0,1:T(8,128)}), f32[256,256]{0,1:T(8,128)}) %all-reduce.16.cloned.1.call-update) | async-done | bytes 262160 | tf_op jit(solution)/shard_map/psum | solution.py:32
  665.1 1.1 copy.8
  666.2 1.0 fusion.12
  667.2 11.7 %cholesky.164 = f32[128,128]{1,0:T(8,128)S(1)} custom-call(f32[128,128]{1,0:T(8,128)S(1)} %cholesky.197), custom_call_target="Cholesky" | custom-call | tf_op jit(solution)/shard_map/jit(cholesky)/cholesky | solution.py:16
  679.6 9.8 %custom-call.15 = f32[1,128,128]{1,2,0:T(8,128)S(1)} custom-call(f32[1,128,128]{2,1,0:T(8,128)S(1)} %get-tuple-element.43), custom_call_target="InvertDiagBlocksLowerTriangular" | custom-call | tf_op jit(solution)/shard_map/jit(cholesky)/cholesky | solution.py:16
  689.9 11.7 %cholesky.181 = f32[128,128]{1,0:T(8,128)S(1)} custom-call(f32[128,128]{1,0:T(8,128)S(1)} %convolution_subtract_fusion.2), custom_call_target="Cholesky" | custom-call | tf_op jit(solution)/shard_map/jit(cholesky)/cholesky | solution.py:16
  703.7 4.3 while.5
  704.5 1.4 bitcast_dynamic-update-slice_fusion.5
  706.5 1.4 bitcast_dynamic-update-slice_fusion.5
  707.9 19.7 %custom-call.16 = f32[2,128,128]{1,2,0:T(8,128)S(1)} custom-call(f32[2,128,128]{2,1,0:T(8,128)S(1)} %get-tuple-element.19), custom_call_target="InvertDiagBlocksLowerTriangular" | custom-call | tf_op jit(solution)/shard_map/triangular_solve/custom-call.0 | solution.py:17
  727.6 1.7 fusion.5
  729.3 2.0 convolution_subtract_fusion
  732.0 2.4 fusion.4
  734.4 64.9 %all-reduce.18.cloned.1.call-done = f32[448,256]{1,0:T(8,128)} async-done(((f32[448,256]{1,0:T(8,128)}), f32[448,256]{1,0:T(8,128)}) %all-reduce.18.cloned.1.call-update) | async-done | bytes 458768 | tf_op jit(solution)/shard_map/psum | solution.py:37
  799.3 1.1 multiply_reduce_fusion
  800.4 75.0 %psum.63 = f32[256]{0:T(256)S(1)} all-reduce(f32[256]{0:T(256)S(1)} %multiply_reduce_fusion), channel_id=1, replica_groups=mesh['row'=8,'col'=32] {'col'}, use_global_device_ids=true, to_apply=%region_13.16 | all-reduce | flops 256 | bytes 2048 | tf_op jit(solution)/shard_map/psum | solution.py:38
  875.5 4.1 multiply_subtract_fusion
  879.6 2.9 convolution_multiply_fusion
  (48 shorter events, 7.3 us)
Async XLA Ops:
  7.2 2.6 copy-start
  7.2 159.5 %all-reduce.8.cloned.1.call-start = ((), (), s32[]{:S(2)}) async-start(), calls=%async_computation | async-start | bytes 2097152 | tf_op jit(solution)/shard_map/psum | solution.py:31
  14.2 216.9 %all-reduce.10.cloned.1.call-start = ((), (), s32[]{:S(2)}) async-start(), calls=%async_computation.1 | async-start | bytes 524288 | tf_op jit(solution)/shard_map/psum | solution.py:32
  170.7 202.9 %all-reduce.12.cloned.1.call-start = ((), (), s32[]{:S(2)}) async-start(), calls=%async_computation.2 | async-start | bytes 917504 | tf_op jit(solution)/shard_map/psum | solution.py:37
  232.9 70.3 %copy-start.1 = (f32[1024,256]{1,0:T(8,128)S(1)}, f32[1024,256]{1,0:T(8,128)}, u32[]{:S(2)}) copy-start(f32[1024,256]{1,0:T(8,128)} %all-reduce.8.cloned.1.call-done) | copy-start | bytes 3145732
  234.1 0.7 copy-start.3
  282.1 0.7 copy-start.4
  308.8 291.9 %all-reduce.14.cloned.1.call-start = ((), (), s32[]{:S(2)}) async-start(), calls=%async_computation.3 | async-start | bytes 2097152 | tf_op jit(solution)/shard_map/psum | solution.py:31
  455.3 209.8 %all-reduce.16.cloned.1.call-start = ((), (), s32[]{:S(2)}) async-start(), calls=%async_computation.4 | async-start | bytes 524288 | tf_op jit(solution)/shard_map/psum | solution.py:32
  604.7 194.6 %all-reduce.18.cloned.1.call-start = ((), (), s32[]{:S(2)}) async-start(), calls=%async_computation.5 | async-start | bytes 917504 | tf_op jit(solution)/shard_map/psum | solution.py:37
  875.5 4.1 copy-start.2
Sparse Core Ops, SparseCore 0:
  14.4 152.2 all-reduce.7
  170.9 60.2 all-reduce.9
  308.9 64.7 all-reduce.11
  455.4 145.1 all-reduce.13
  604.9 60.2 all-reduce.15
  734.5 64.7 all-reduce.17
where the time goes:
time: 896 us; the launch traced here: 890 us
  waiting for transfers between devices  548 us (61%)
  blocking collectives  150 us (17%)
  other arithmetic  118 us (13%)
  matrix products  40.5 us (5%)
  between operations  17.4 us (2%)
  local copies, waits for them, and re-layouts  14.8 us (2%)
    psum x2, waiting for transfers between devices, on_device(): left = lax.psum(partial_value, 'col')  298 us
    psum x2, blocking collectives, on_device(): squares = lax.psum(jnp.sum(carried * carried, axis=0), 'col')  150 us
    psum x2, waiting for transfers between devices, on_device(): carried = lax.psum(partial_value, 'row')  130 us
    psum x2, waiting for transfers between devices, on_device(): gram = lax.psum(gram_of(left), 'row')  120 us
    another operation x13, other arithmetic, solve_left(): lower = jnp.linalg.cholesky(gram)  69.2 us
    another operation x5, other arithmetic, solve_left(): lax.linalg.triangular_solve(lower, left, left_side=False, lower=True, tra...  41.9 us
  transfers between devices with their start and end apart: 6, of which 6 were waited for; matrix products, arithmetic and copies ran while one was open for 0% of the time, Pallas kernels for 0%

commit v1 on v0

v1 whole, which is shorter than its diff:
```python
import jax
import jax.numpy as jnp
from jax import lax
from jax.experimental import pallas as pl
from jax.sharding import PartitionSpec as P

D = 8192
FF = 14336
RANK = 256
MU = 0.95
EPS = 1e-06

HIGH = lax.Precision.HIGH
HIGHEST = lax.Precision.HIGHEST

X_GROUPS = [[z * 4 + x for x in range(4)] for z in range(8)]
Z_GROUPS = [[z * 4 + x for z in range(8)] for x in range(4)]
Y_GROUPS = [[y * 2 + c for y in range(4)] for c in range(2)]
OTHER_CORE = [(i, i ^ 1) for i in range(8)]


def dot(a, b, contract, precision):
    return lax.dot_general(
        a, b, (contract, ((), ())), precision=precision, preferred_element_type=jnp.float32
    )


def factor(block):
    size = block.shape[0]
    count = size // 8
    groups = [block[8 * g : 8 * g + 8, :] for g in range(count)]
    lane = lax.broadcasted_iota(jnp.int32, (8, size), 1)
    sub = lax.broadcasted_iota(jnp.int32, (8, size), 0)
    for j in range(size):
        first, r = divmod(j, 8)
        here = lane == j
        row = jnp.broadcast_to(groups[first][r : r + 1, :], (8, size))
        inverse = 1.0 / jnp.broadcast_to(row[:, j : j + 1], (8, size))
        scaled = jnp.where(here, 1.0, row) * inverse
        for g in range(first, count):
            old = groups[g]
            multiplier = jnp.broadcast_to(old[:, j : j + 1], (8, size))
            new = jnp.where(here, 0.0, old) - multiplier * scaled
            groups[g] = jnp.where(sub > r, new, old) if g == first else new
    rows = []
    for g in range(count):
        row = sub + 8 * g
        pivot = jnp.sum(jnp.where(lane == row, groups[g], 0.0), axis=1, keepdims=True)
        unit = jnp.where(lane < row, groups[g], jnp.where(lane == row, 1.0, 0.0))
        rows.append(unit * lax.rsqrt(pivot))
    return jnp.concatenate(rows, 0)


def cholesky_inverse_kernel(gram_ref, out_ref):
    h = RANK // 2
    top = factor(gram_ref[0:h, 0:h])
    lower = dot(gram_ref[h:, 0:h], top, ((1,), (1,)), HIGHEST)
    bottom = factor(gram_ref[h:, h:] - dot(lower, lower, ((1,), (1,)), HIGHEST))
    corner = dot(bottom, dot(lower, top, ((1,), (0,)), HIGHEST), ((1,), (0,)), HIGHEST)
    out_ref[0:h, 0:h] = top
    out_ref[0:h, h:] = jnp.zeros((h, h), jnp.float32)
    out_ref[h:, 0:h] = -corner
    out_ref[h:, h:] = bottom


def cholesky_inverse(gram):
    return pl.pallas_call(
        cholesky_inverse_kernel, out_shape=jax.ShapeDtypeStruct((RANK, RANK), jnp.float32)
    )(gram)


def scatter_sum(value, axis, groups):
    n = len(groups[0])
    value = lax.all_to_all(value, axis, 0, 0, tiled=True, axis_index_groups=groups)
    return jnp.sum(value.reshape(n, -1, RANK), axis=0)


def gather(value, axis, groups):
    n = len(groups[0])
    value = jnp.tile(value, (n, 1))
    return lax.all_to_all(value, axis, 0, 0, tiled=True, axis_index_groups=groups)


def sum_over_col(value):
    with jax.named_scope("sum_over_col"):
        value = scatter_sum(value, "col", X_GROUPS)
        value = scatter_sum(value, "col", Z_GROUPS)
        value = gather(value, "col", Z_GROUPS)
        return gather(value, "col", X_GROUPS)


def sum_over_row(value):
    with jax.named_scope("sum_over_row"):
        half = value.shape[0] // 2
        core = lax.axis_index("row") % 2
        mine = lax.dynamic_slice_in_dim(value, core * half, half)
        theirs = lax.dynamic_slice_in_dim(value, (1 - core) * half, half)
        value = mine + lax.ppermute(theirs, "row", OTHER_CORE)
        value = scatter_sum(value, "row", Y_GROUPS)
        value = gather(value, "row", Y_GROUPS)
        other = lax.ppermute(value, "row", OTHER_CORE)
        first = jnp.where(core == 0, value, other)
        second = jnp.where(core == 0, other, value)
        return jnp.concatenate([first, second], 0)


def on_device(momentum, gradient, right_factor):
    cols = momentum.shape[1]
    buffer = momentum + gradient
    left = sum_over_col(dot(buffer, right_factor, ((1,), (0,)), HIGH))
    carried = dot(buffer, left, ((0,), (0,)), HIGH)
    gram = dot(left, left, ((0,), (0,)), HIGHEST)
    both = sum_over_row(jnp.concatenate([carried, gram], 0))
    carried, gram = both[:cols], both[cols:]
    inverse = cholesky_inverse(gram)
    carried = dot(carried, inverse, ((1,), (1,)), HIGHEST)
    left = dot(left, inverse, ((1,), (1,)), HIGHEST)
    product = sum_over_col(dot(buffer, carried, ((1,), (0,)), HIGH))
    squares = jnp.sum(left * product, axis=0, keepdims=True)
    carried = dot(buffer, product, ((0,), (0,)), HIGH)
    gram = dot(product, product, ((0,), (0,)), HIGHEST)
    both = sum_over_row(
        jnp.concatenate([carried, gram, jnp.pad(squares, ((0, 63), (0, 0)))], 0)
    )
    carried, gram, squares = both[:cols], both[cols : cols + RANK], both[cols + RANK]
    scale = 1.0 / jnp.sqrt(jnp.maximum(squares, 0.0) + EPS)
    inverse = cholesky_inverse(gram * scale[:, None] * scale[None, :]) * scale[None, :]
    left = dot(product, inverse, ((1,), (1,)), HIGHEST)
    carried = dot(carried, inverse, ((1,), (1,)), HIGHEST)
    squares = jnp.sum(carried * carried, axis=0, keepdims=True)
    squares = lax.all_to_all(jnp.tile(squares, (32, 1)), "col", 0, 0, tiled=True)
    squares = jnp.sum(squares, axis=0, keepdims=True)
    factor_ = jnp.float32((D * FF / RANK) ** 0.5)
    right = carried * (factor_ / jnp.sqrt(squares + EPS))
    momentum_next = buffer - (1.0 - MU) * dot(left, carried, ((1,), (1,)), HIGH)
    update = dot(left, right, ((1,), (1,)), HIGH)
    return (momentum_next, update)


def solution(mesh):
    return jax.shard_map(
        on_device,
        mesh=mesh,
        in_specs=(P("row", "col"), P("row", "col"), P("col", None)),
        out_specs=(P("row", "col"), P("row", "col")),
        check_vma=False,
    )
```

time: 896 us -> 306 us (0.34)
  waiting for transfers between devices: 548 us -> 37.7 us
  other arithmetic: 118 us -> 11 us
  Pallas kernels: 0 us -> 73.5 us
  matrix products: 40.5 us -> 23.7 us
  between operations: 17.4 us -> 0.91 us
  starting transfers between devices: 0.92 us -> 11.1 us
  blocking collectives: 150 us -> 140 us
    psum x6 -> x0, waiting for transfers between devices: 547 us -> none  [the longest x2 298 us: on_device(): left = lax.psum(partial_value, 'col')]
    psum x2 -> x0, blocking collectives: 150 us -> none  [on_device(): squares = lax.psum(jnp.sum(carried * carried, axis=0), 'col')]
    all_to_all x0 -> x10, blocking collectives: none -> 140 us  [the longest x6 94.4 us: scatter_sum(): lax.all_to_all(value, axis, 0, 0, tiled=True, axis_index_groups=groups)]
    another operation x18 -> x0, other arithmetic: 111 us -> none  [the longest x13 69.2 us: solve_left(): lower = jnp.linalg.cholesky(gram)]
    pallas_call x0 -> x2, Pallas kernels: none -> 73.5 us  [cholesky_inverse(): pl.pallas_call(cholesky_inverse_kernel, out_shape=jax.ShapeDtypeStruct((R...]
    all_to_all x0 -> x3, waiting for transfers between devices: none -> 30.3 us  [the longest x2 23.7 us: gather(): lax.all_to_all(value, axis, 0, 0, tiled=True, axis_index_groups=groups)]
    all_to_all x0 -> x3, starting transfers between devices: none -> 11.1 us  [the longest x2 7.26 us: gather(): lax.all_to_all(value, axis, 0, 0, tiled=True, axis_index_groups=groups)]
    another operation x10 -> x0, matrix products: 10.7 us -> none  [the longest x6 7.44 us: solve_left(): lax.linalg.triangular_solve(lower, left, left_side=False, lower=True, tra...]
  transfers between devices with their start and end apart: 6 -> 7, of which waited for: 6 -> 7; matrix products, arithmetic and copies ran while one was open for 0% -> 1% of each run, Pallas kernels for 0% -> 0%
where the time goes in v1:
time: 306 us; the launch traced here: 304 us
  blocking collectives  140 us (46%)
  Pallas kernels  73.5 us (24%)
  waiting for transfers between devices  37.7 us (12%)
  matrix products  23.7 us (8%)
  starting transfers between devices  11.1 us (4%)
  other arithmetic  11 us (4%)
  local copies, waits for them, and re-layouts  5.95 us (2%)
    all_to_all x6, blocking collectives, scatter_sum(): lax.all_to_all(value, axis, 0, 0, tiled=True, axis_index_groups=groups)  94.4 us
    pallas_call x2, Pallas kernels, cholesky_inverse(): pl.pallas_call(cholesky_inverse_kernel, out_shape=jax.ShapeDtypeStruct((R...  73.5 us
    all_to_all x4, blocking collectives, gather(): lax.all_to_all(value, axis, 0, 0, tiled=True, axis_index_groups=groups)  45.6 us
    all_to_all x2, waiting for transfers between devices, gather(): lax.all_to_all(value, axis, 0, 0, tiled=True, axis_index_groups=groups)  23.7 us
    dot_general x12, matrix products, dot(): lax.dot_general(a, b, (contract, ((), ())), precision=precision, preferre...  23.7 us
    all_to_all x2, starting transfers between devices, gather(): lax.all_to_all(value, axis, 0, 0, tiled=True, axis_index_groups=groups)  7.26 us
    all_to_all x1, waiting for transfers between devices, on_device(): lax.all_to_all(jnp.tile(squares, (32, 1)), 'col', 0, 0, tiled=True)  6.55 us
  transfers between devices with their start and end apart: 7, of which 7 were waited for; matrix products, arithmetic and copies ran while one was open for 1% of the time, Pallas kernels for 0%

profile of v1, /device:TPU:8, one launch (start us, length us, event | category | flops | bytes accessed | tf_op | source)
XLA Modules:
  0.0 304.0 jit_solution(13445643885444867913)
XLA Ops:
  0.6 2.6 add.51
  3.2 1.8 fusion.21
  5.0 19.2 %all_to_all.108 = f32[4,256,256]{2,1,0:T(8,128)S(1)} all-to-all(f32[4,256,256]{2,1,0:T(8,128)S(1)} %bitcast.47), channel_id=1, replica_groups={{0,1,2,3},{4,5,6,7},{8,9,10,11},{12,13,14,15},{16,17,18,19},{20,21,22,2..., dimensions={0} | all-to-all | bytes 2097152 | tf_op jit(solution)/shard_map/sum_over_col/all_to_all | solution.py:74
  24.2 0.8 reduce_sum.81
  25.0 19.1 %all_to_all.109 = f32[8,32,256]{2,1,0:T(8,128)S(1)} all-to-all(f32[8,32,256]{2,1,0:T(8,128)} %bitcast.52), channel_id=1, replica_groups={{0,4,8,12,16,20,24,28},{1,5,9,13,17,21,25,29},{2,6,10,14,18,22,26,30},{..., dimensions={0} | all-to-all | bytes 524288 | tf_op jit(solution)/shard_map/sum_over_col/all_to_all | solution.py:74
  44.2 12.9 %all_to_all.110 = f32[8,32,256]{2,1,0:T(8,128)S(1)} all-to-all(f32[8,32,256]{2,1,0:T(8,128)S(1)} %tile.18), channel_id=1, replica_groups={{0,4,8,12,16,20,24,28},{1,5,9,13,17,21,25,29},{2,6,10,14,18,22,26,30},{..., dimensions={0} | all-to-all | bytes 524288 | tf_op jit(solution)/shard_map/sum_over_col/all_to_all | solution.py:81
  57.1 1.1 tile.20
  58.1 3.5 %all-to-all-start.3 = ((f32[4,256,256]{2,1,0:T(8,128)}), f32[4,256,256]{2,1,0:T(8,128)S(1)}, u32[]{:S(2)}, u32[]{:S(2)}) async-start(f32[4,256,256]{2,1,0:T(8,128)} %tile.20), calls=%async_computation.3 | async-start | bytes 2097152 | tf_op jit(solution)/shard_map/sum_over_col/all_to_all | solution.py:81
  61.7 11.4 %all-to-all-done.3 = f32[4,256,256]{2,1,0:T(8,128)S(1)} async-done(((f32[4,256,256]{2,1,0:T(8,128)}), f32[4,256,256]{2,1,0:T(8,128)S(1)}, u32[]{:S(2)}, u32[]{:S(2)}) %all-to-all-start.3) | async-done | bytes 1048608 | tf_op jit(solution)/shard_map/sum_over_col/all_to_all | solution.py:81
  73.1 0.9 fusion.22
  74.1 1.8 convolution_bitcast_fusion.1
  75.9 0.8 fusion.7
  76.8 1.9 collective-permute-done
  78.6 1.1 fusion.9
  79.7 11.3 %all_to_all.111 = f32[4,88,256]{2,1,0:T(8,128)S(1)} all-to-all(f32[4,88,256]{2,1,0:T(8,128)S(1)} %bitcast.51), channel_id=1, replica_groups={{0,64,128,192},{32,96,160,224},{1,65,129,193},{33,97,161,225},{2,66,130..., dimensions={0} | all-to-all | bytes 720896 | tf_op jit(solution)/shard_map/sum_over_row/all_to_all | solution.py:74
  91.1 9.6 %all_to_all.112 = f32[4,88,256]{2,1,0:T(8,128)S(1)} all-to-all(f32[4,88,256]{2,1,0:T(8,128)S(1)} %tile.21), channel_id=1, replica_groups={{0,64,128,192},{32,96,160,224},{1,65,129,193},{33,97,161,225},{2,66,130..., dimensions={0} | all-to-all | bytes 720896 | tf_op jit(solution)/shard_map/sum_over_row/all_to_all | solution.py:81
  100.7 1.8 collective-permute-done.1
  102.5 1.0 broadcast_select_fusion.3
  104.2 36.8 %shard_map.50 = f32[256,256]{1,0:T(8,128)} custom-call(f32[256,256]{1,0:T(8,128)} %slice.20.gram_ref), custom_call_target="tpu_custom_call" | custom-call | tf_op jit(solution)/shard_map/pallas_call | solution.py:67
  141.0 1.5 fusion.3
  142.5 1.8 fusion.23
  144.4 18.1 %all_to_all.113 = f32[4,256,256]{2,1,0:T(8,128)S(1)} all-to-all(f32[4,256,256]{2,1,0:T(8,128)S(1)} %bitcast.46), channel_id=1, replica_groups={{0,1,2,3},{4,5,6,7},{8,9,10,11},{12,13,14,15},{16,17,18,19},{20,21,22,2..., dimensions={0} | all-to-all | bytes 2097152 | tf_op jit(solution)/shard_map/sum_over_col/all_to_all | solution.py:74
  162.5 0.8 reduce_sum.84
  163.2 14.9 %all_to_all.114 = f32[8,32,256]{2,1,0:T(8,128)S(1)} all-to-all(f32[8,32,256]{2,1,0:T(8,128)} %bitcast.54), channel_id=1, replica_groups={{0,4,8,12,16,20,24,28},{1,5,9,13,17,21,25,29},{2,6,10,14,18,22,26,30},{..., dimensions={0} | all-to-all | bytes 524288 | tf_op jit(solution)/shard_map/sum_over_col/all_to_all | solution.py:74
  178.2 12.9 %all_to_all.115 = f32[8,32,256]{2,1,0:T(8,128)S(1)} all-to-all(f32[8,32,256]{2,1,0:T(8,128)S(1)} %tile.22), channel_id=1, replica_groups={{0,4,8,12,16,20,24,28},{1,5,9,13,17,21,25,29},{2,6,10,14,18,22,26,30},{..., dimensions={0} | all-to-all | bytes 524288 | tf_op jit(solution)/shard_map/sum_over_col/all_to_all | solution.py:81
  191.1 1.1 tile.24
  192.2 3.7 %all-to-all-start.9 = ((f32[4,256,256]{2,1,0:T(8,128)}), f32[4,256,256]{2,1,0:T(8,128)S(1)}, u32[]{:S(2)}, u32[]{:S(2)}) async-start(f32[4,256,256]{2,1,0:T(8,128)} %tile.24), calls=%async_computation.9 | async-start | bytes 2097152 | tf_op jit(solution)/shard_map/sum_over_col/all_to_all | solution.py:81
  195.9 12.3 %all-to-all-done.9 = f32[4,256,256]{2,1,0:T(8,128)S(1)} async-done(((f32[4,256,256]{2,1,0:T(8,128)}), f32[4,256,256]{2,1,0:T(8,128)S(1)}, u32[]{:S(2)}, u32[]{:S(2)}) %all-to-all-start.9) | async-done | bytes 1048608 | tf_op jit(solution)/shard_map/sum_over_col/all_to_all | solution.py:81
  208.2 2.3 fusion
  210.5 0.9 fusion.24
  211.4 1.8 convolution_bitcast_fusion
  213.4 0.9 copy-done.4
  214.2 0.8 constant_dynamic-slice_fusion
  215.0 2.1 collective-permute-done.2
  217.1 1.2 dynamic-slice_add_fusion
  218.2 11.7 %all_to_all.116 = f32[4,96,256]{2,1,0:T(8,128)} all-to-all(f32[4,96,256]{2,1,0:T(8,128)S(1)} %bitcast.49), channel_id=1, replica_groups={{0,64,128,192},{32,96,160,224},{1,65,129,193},{33,97,161,225},{2,66,130..., dimensions={0} | all-to-all | bytes 786432 | tf_op jit(solution)/shard_map/sum_over_row/all_to_all | solution.py:74
  230.0 1.0 reduce_sum.87
  231.0 10.2 %all_to_all.117 = f32[4,96,256]{2,1,0:T(8,128)S(1)} all-to-all(f32[4,96,256]{2,1,0:T(8,128)S(1)} %tile.25), channel_id=1, replica_groups={{0,64,128,192},{32,96,160,224},{1,65,129,193},{33,97,161,225},{2,66,130..., dimensions={0} | all-to-all | bytes 786432 | tf_op jit(solution)/shard_map/sum_over_row/all_to_all | solution.py:81
  241.2 1.7 collective-permute-done.3
  243.0 0.8 broadcast_select_fusion
  244.5 0.8 fusion.10.gram_ref
  245.3 36.8 %shard_map.51 = f32[256,256]{1,0:T(8,128)} custom-call(f32[256,256]{1,0:T(8,128)} %fusion.10.gram_ref), custom_call_target="tpu_custom_call" | custom-call | tf_op jit(solution)/shard_map/pallas_call | solution.py:67
  282.1 3.0 fusion.12
  285.1 1.3 multiply_reduce_fusion
  287.1 3.8 %all-to-all-start.12 = ((f32[32,1,256]{2,1,0:T(1,128)}), f32[32,1,256]{2,1,0:T(1,128)S(1)}, u32[]{:S(2)}, u32[]{:S(2)}) async-start(f32[32,1,256]{2,1,0:T(1,128)} %tile.26), calls=%async_computation.12 | async-start | bytes 65536 | tf_op jit(solution)/shard_map/all_to_all | solution.py:131
  291.0 3.2 %multiply_subtract_fusion = f32[1024,448]{0,1:T(8,128)} fusion(f32[1024,448]{0,1:T(8,128)S(1)} %add.51, f32[1024,256]{1,0:T(8,128)S(1)} %copy-done.2, f32[448,256]{1,0:T(8,128)} %get-tuple-element.7), kind=kOutput, calls=%fused_computation | convolution fusion | flops 705560576 | bytes 5177344 | tf_op jit(solution)/shard_map/dot_general | solution.py:23
  294.2 6.5 %all-to-all-done.12 = f32[32,1,256]{2,1,0:T(1,128)S(1)} async-done(((f32[32,1,256]{2,1,0:T(1,128)}), f32[32,1,256]{2,1,0:T(1,128)S(1)}, u32[]{:S(2)}, u32[]{:S(2)}) %all-to-all-start.12) | async-done | bytes 32800 | tf_op jit(solution)/shard_map/all_to_all | solution.py:131
  300.8 3.2 %fusion.5 = f32[1024,448]{0,1:T(8,128)} fusion(f32[1024,256]{1,0:T(8,128)S(1)} %copy-done.2, f32[448,256]{1,0:T(8,128)} %get-tuple-element.7, f32[256]{0:T(256)S(1)} %rsqrt_multiply_fusion), kind=kOutput, calls=%fused_computation.17 | convolution fusion | flops 704757760 | bytes 3343360 | tf_op jit(solution)/shard_map/dot_general | solution.py:23
  (36 shorter events, 2.4 us)
Async XLA Ops:
  0.6 2.6 copy-start
  58.1 15.0 %all-to-all-start.3 = ((f32[4,256,256]{2,1,0:T(8,128)}), f32[4,256,256]{2,1,0:T(8,128)S(1)}, u32[]{:S(2)}, u32[]{:S(2)}) async-start(f32[4,256,256]{2,1,0:T(8,128)} %tile.20), calls=%async_computation.3 | async-start | bytes 2097152 | tf_op jit(solution)/shard_map/sum_over_col/all_to_all | solution.py:81
  73.1 2.8 copy-start.1
  74.0 2.7 copy-start.3
  75.9 0.8 copy-start.8
  76.8 1.9 collective-permute-start
  100.7 1.8 collective-permute-start.1
  192.2 16.1 %all-to-all-start.9 = ((f32[4,256,256]{2,1,0:T(8,128)}), f32[4,256,256]{2,1,0:T(8,128)S(1)}, u32[]{:S(2)}, u32[]{:S(2)}) async-start(f32[4,256,256]{2,1,0:T(8,128)} %tile.24), calls=%async_computation.9 | async-start | bytes 2097152 | tf_op jit(solution)/shard_map/sum_over_col/all_to_all | solution.py:81
  213.3 0.9 copy-start.4
  215.0 2.1 collective-permute-start.2
  241.2 1.7 collective-permute-start.3
  243.8 0.7 copy-start.5
  282.1 3.0 %copy-start.6 = (f32[384,256]{1,0:T(8,128)S(1)}, f32[384,256]{1,0:T(8,128)}, u32[]{:S(2)}) copy-start(f32[384,256]{1,0:T(8,128)} %copy-done.5) | copy-start | bytes 1179652
  282.1 3.0 %copy-start.7 = (f32[256,256]{1,0:T(8,128)S(1)}, f32[256,256]{1,0:T(8,128)}, u32[]{:S(2)}) copy-start(f32[256,256]{1,0:T(8,128)} %shard_map.51) | copy-start | bytes 786436
  282.1 3.0 %copy-start.9 = (f32[384,256]{1,0:T(8,128)S(1)}, f32[384,256]{1,0:T(8,128)}, u32[]{:S(2)}) copy-start(f32[384,256]{1,0:T(8,128)} %get-tuple-element.2) | copy-start | bytes 1179652
  285.1 5.8 %copy-start.2 = (f32[1024,256]{1,0:T(8,128)S(1)}, f32[1024,256]{1,0:T(8,128)}, u32[]{:S(2)}) copy-start(f32[1024,256]{1,0:T(8,128)} %fusion.12) | copy-start | bytes 3145732
  287.1 13.6 %all-to-all-start.12 = ((f32[32,1,256]{2,1,0:T(1,128)}), f32[32,1,256]{2,1,0:T(1,128)S(1)}, u32[]{:S(2)}, u32[]{:S(2)}) async-start(f32[32,1,256]{2,1,0:T(1,128)} %tile.26), calls=%async_computation.12 | async-start | bytes 65536 | tf_op jit(solution)/shard_map/all_to_all | solution.py:131

commit v2 on v0

v2 whole, which is shorter than its diff:
```python
import functools

import jax
import jax.numpy as jnp
from jax import lax
from jax.experimental import pallas as pl
from jax.experimental.pallas import tpu as pltpu
from jax.sharding import PartitionSpec as P

D = 8192
FF = 14336
RANK = 256
MU = 0.95
EPS = 1e-06
ROWS = 1024
COLS = 448
BLOCK = ROWS // 4
FIRST = COLS + RANK
GRAM = RANK + 16
PART = COLS // 8

HIGHEST = lax.Precision.HIGHEST
LIMIT = 24 * 1024 * 1024

X_SHIFTS = [[(i, i // 4 * 4 + (i + k) % 4) for i in range(32)] for k in (1, 2, 3)]
Z_GROUPS = [[z * 4 + x for z in range(8)] for x in range(4)]
Y_GROUPS = [[y * 2 + c for y in range(4)] for c in range(2)]
Y_SHIFTS = [[(i, (i // 2 + k) % 4 * 2 + i % 2) for i in range(8)] for k in (1, 2, 3)]
OTHER_CORE = [(i, i ^ 1) for i in range(8)]

VMEM = pl.BlockSpec(memory_space=pltpu.VMEM)
SMEM = pl.BlockSpec(memory_space=pltpu.SMEM)
HBM = pl.BlockSpec(memory_space=pltpu.HBM)


def shape(*dims):
    return jax.ShapeDtypeStruct(dims, jnp.float32)


def scratch(*dims):
    return pltpu.VMEM(dims, jnp.float32)


def params(**more):
    return pltpu.CompilerParams(vmem_limit_bytes=LIMIT, **more)


def cost(flops):
    return pl.CostEstimate(flops=flops, bytes_accessed=1_000_000, transcendentals=0)


def dot(a, b, contract, precision=HIGHEST):
    return lax.dot_general(
        a, b, (contract, ((), ())), precision=precision, preferred_element_type=jnp.float32
    )


def split(value):
    high = value.astype(jnp.bfloat16)
    return high, (value - high.astype(jnp.float32)).astype(jnp.bfloat16)


def dot3(a, b, contract):
    (a0, a1), (b0, b1) = a, b
    one = functools.partial(dot, contract=contract, precision=None)
    return one(a0, b0) + (one(a0, b1) + one(a1, b0))


def full(value, size):
    return jnp.broadcast_to(value, (8, size))


def factor(block):
    size = block.shape[0]
    count = size // 8
    groups = [block[8 * g : 8 * g + 8, :] for g in range(count)]
    lane = lax.broadcasted_iota(jnp.int32, (8, size), 1)
    sub = lax.broadcasted_iota(jnp.int32, (8, size), 0)
    pivots = []
    for p in range(count):
        base = 8 * p
        own = groups[p]
        rows = [full(own[k : k + 1, :], size) for k in range(8)]
        columns = [full(own[:, base + i : base + i + 1], size) for i in range(8)]
        s = [[full(columns[i][k : k + 1, :], size) for i in range(k + 1)] for k in range(8)]
        inverse = [None] * 8
        low = [[None] * 8 for _ in range(8)]
        for j in range(0, 8, 2):
            a, b, c = s[j][j], s[j + 1][j], s[j + 1][j + 1]
            det = a * c - b * b
            inverse_det = 1.0 / det
            inverse[j] = 1.0 / a
            inverse[j + 1] = a * inverse_det
            low[j + 1][j] = b * inverse[j]
            before = {k: (s[k][j], s[k][j + 1]) for k in range(j + 2, 8)}
            for k in range(j + 2, 8):
                u, v = before[k]
                w0 = (c * u - b * v) * inverse_det
                w1 = (a * v - b * u) * inverse_det
                for i in range(j + 2, k + 1):
                    s[k][i] = s[k][i] - (w0 * before[i][0] + w1 * before[i][1])
                low[k][j] = u * inverse[j]
                low[k][j + 1] = w1
                s[k][j + 1] = v - low[k][j] * b
            s[j + 1][j + 1] = det * inverse[j]
        for j in range(8):
            here = lane == base + j
            row = jnp.where(here, 1.0, rows[j])
            for k in range(j + 1, 8):
                rows[k] = jnp.where(here, 0.0, rows[k]) - low[k][j] * row
        inside = (lane >= base) & (lane < base + 8)
        tails = [
            jnp.where(inside & (lane > base + j), 0.0, jnp.where(lane == base + j, 1.0, rows[j]))
            for j in range(8)
        ]
        for g in range(p + 1, count):
            old = groups[g]
            values = [full(old[:, base + i : base + i + 1], size) for i in range(8)]
            terms = []
            for j in range(8):
                multiplier = values[j] * inverse[j]
                for i in range(j + 1, 8):
                    values[i] = values[i] - multiplier * s[i][j]
                terms.append(multiplier * tails[j])
            while len(terms) > 1:
                terms = [terms[i] + terms[i + 1] for i in range(0, len(terms), 2)]
            groups[g] = jnp.where(inside, 0.0, old) - terms[0]
        merged, pivot = rows[0], s[0][0]
        for k in range(1, 8):
            merged = jnp.where(sub == k, rows[k], merged)
            pivot = jnp.where(sub == k, s[k][k], pivot)
        groups[p] = merged
        pivots.append(pivot)
    out = []
    for g in range(count):
        row = sub + 8 * g
        unit = jnp.where(lane < row, groups[g], jnp.where(lane == row, 1.0, 0.0))
        out.append(unit * lax.rsqrt(pivots[g]))
    return jnp.concatenate(out, 0)


def tile_of(position):
    return pl.ds(pl.multiple_of(position * BLOCK, BLOCK), BLOCK)


def half_of(position, size):
    return pl.ds(pl.multiple_of(position * size, 8), size)


def forward_blocks(x, buffer_ref, factor, out_refs):
    factor = split(factor)
    for k in range(4):
        tile = split(buffer_ref[:, tile_of(lax.rem(x + k, 4))])
        out_refs[k][...] = dot3(tile, factor, ((0,), (0,)))


def start_kernel(x_ref, buffer_ref, right_ref, *out_refs):
    forward_blocks(x_ref[0], buffer_ref, right_ref[...], out_refs)


def start(x, buffer, right):
    return pl.pallas_call(
        start_kernel,
        in_specs=[SMEM, VMEM, VMEM],
        out_specs=[VMEM] * 4,
        out_shape=[shape(BLOCK, RANK)] * 4,
        compiler_params=params(),
        name="start",
    )(x, buffer, right)


def forward_kernel(x_ref, core_ref, buffer_ref, half_ref, other_ref, *rest):
    *out_refs, gram_ref, both = rest
    core = core_ref[0]
    both[half_of(core, FIRST // 2), :] = half_ref[...]
    both[half_of(1 - core, FIRST // 2), :] = other_ref[...]
    gram_ref[...] = both[COLS:FIRST, :]
    forward_blocks(x_ref[0], buffer_ref, both[0:COLS, :], out_refs)


def forward(x, core, buffer, half, other):
    return pl.pallas_call(
        forward_kernel,
        in_specs=[SMEM, SMEM, VMEM, VMEM, VMEM],
        out_specs=[VMEM] * 5,
        out_shape=[shape(BLOCK, RANK)] * 5,
        scratch_shapes=[scratch(FIRST, RANK)],
        compiler_params=params(),
        name="forward",
    )(x, core, buffer, half, other)


def backward_kernel(x_ref, core_ref, buffer_ref, *rest):
    *left_refs, mine_ref, theirs_ref, left, both = rest
    x, core = x_ref[0], core_ref[0]
    for k in range(4):
        left[tile_of(lax.rem(x + 4 - k, 4)), :] = left_refs[k][...]
    both[0:COLS, :] = dot3(split(buffer_ref[...]), split(left[...]), ((1,), (0,)))
    both[COLS:FIRST, :] = dot(left[...], left[...], ((0,), (0,)))
    mine_ref[...] = both[half_of(core, FIRST // 2), :]
    theirs_ref[...] = both[half_of(1 - core, FIRST // 2), :]


def backward(x, core, buffer, left):
    return pl.pallas_call(
        backward_kernel,
        in_specs=[SMEM, SMEM] + [VMEM] * 5,
        out_specs=[VMEM] * 2,
        out_shape=[shape(FIRST // 2, RANK)] * 2,
        scratch_shapes=[scratch(ROWS, RANK), scratch(FIRST, RANK)],
        compiler_params=params(),
        name="backward",
    )(x, core, buffer, *left)


def prepare_kernel(x_ref, inverse_ref, *rest):
    *left_refs, old_ref = rest
    x = x_ref[0]
    inverse = split(inverse_ref[...])
    for k in range(4):
        place = tile_of(lax.rem(x + 4 - k, 4))
        old_ref[place, :] = dot3(split(left_refs[k][...]), inverse, ((1,), (1,)))


def prepare(x, inverse, left):
    return pl.pallas_call(
        prepare_kernel,
        in_specs=[SMEM] + [VMEM] * 5,
        out_specs=VMEM,
        out_shape=shape(ROWS, RANK),
        cost_estimate=cost(2_000_000_000),
        compiler_params=params(),
        name="prepare",
    )(x, inverse, *left)


def solve_kernel(x_ref, core_ref, buffer_ref, inverse_ref, old_ref, *rest):
    product_refs = rest[0:4]
    mine_ref, theirs_ref, out_ref, carried, gram = rest[4:]
    x, core = x_ref[0], core_ref[0]
    for k in range(4):
        place = tile_of(lax.rem(x + 4 - k, 4))
        out_ref[place, :] = dot(product_refs[k][...], inverse_ref[...], ((1,), (1,)))
    product = out_ref[...]
    carried[...] = dot3(split(buffer_ref[...]), split(product), ((1,), (0,)))
    gram[0:RANK, :] = dot(product, product, ((0,), (0,)))
    gram[RANK:GRAM, :] = jnp.zeros((GRAM - RANK, RANK), jnp.float32)
    gram[RANK : RANK + 1, :] = jnp.sum(old_ref[...] * product, axis=0, keepdims=True)
    for half_ref, position in ((mine_ref, core), (theirs_ref, 1 - core)):
        half_ref[0 : GRAM // 2, :] = gram[half_of(position, GRAM // 2), :]
        half_ref[GRAM // 2 :, :] = carried[half_of(position, COLS // 2), :]


def solve(x, core, buffer, inverse, old, product):
    return pl.pallas_call(
        solve_kernel,
        in_specs=[SMEM, SMEM] + [VMEM] * 7,
        out_specs=[VMEM] * 3,
        out_shape=[shape(GRAM // 2 + COLS // 2, RANK)] * 2 + [shape(ROWS, RANK)],
        scratch_shapes=[scratch(COLS, RANK), scratch(GRAM, RANK)],
        compiler_params=params(),
        name="solve",
    )(x, core, buffer, inverse, old, *product)


def cholesky_inverse(gram_ref, out_ref, block, corner):
    h = RANK // 2
    block[...] = gram_ref[0:h, 0:h]

    def step(k, _):
        inverse = factor(block[...])
        out_ref[half_of(k, h), 0:h] = inverse

        @pl.when(k == 0)
        def _():
            lower = dot(gram_ref[h:, 0:h], inverse, ((1,), (1,)))
            block[...] = gram_ref[h:, h:] - dot(lower, lower, ((1,), (1,)))
            corner[...] = dot(lower, inverse, ((1,), (0,)))

        return 0

    lax.fori_loop(0, 2, step, 0)
    bottom = out_ref[h:, 0:h]
    out_ref[h:, 0:h] = -dot(bottom, corner[...], ((1,), (0,)))
    out_ref[h:, h:] = bottom
    out_ref[0:h, h:] = jnp.zeros((h, h), jnp.float32)


def first_inverse(gram):
    return pl.pallas_call(
        cholesky_inverse,
        in_specs=[VMEM],
        out_specs=VMEM,
        out_shape=shape(RANK, RANK),
        scratch_shapes=[scratch(RANK // 2, RANK // 2)] * 2,
        cost_estimate=cost(10_000_000_000),
        compiler_params=params(),
        name="first_inverse",
    )(gram)


def second_kernel(core_ref, half_ref, other_ref, out_ref, whole, gram, inverse, block, corner):
    core = core_ref[0]
    whole[half_of(core, GRAM // 2), :] = half_ref[0 : GRAM // 2, :]
    whole[half_of(1 - core, GRAM // 2), :] = other_ref[0 : GRAM // 2, :]
    scale = 1.0 / jnp.sqrt(jnp.maximum(whole[RANK : RANK + 1, :], 0.0) + EPS)
    gram[...] = (whole[0:RANK, :] * scale).T * scale
    cholesky_inverse(gram, inverse, block, corner)
    h, q = RANK // 2, RANK // 4
    out_ref[0:h, :] = inverse[h:, :] * scale
    out_ref[h:, 0:h] = inverse[0:q, 0:h] * scale[:, 0:h]
    out_ref[h:, h:] = inverse[q:h, 0:h] * scale[:, 0:h]


def times_inverse(value, packed):
    h = RANK // 2
    top = jnp.concatenate([packed[h:, 0:h], packed[h:, h:]], 0)
    left = dot(value[:, 0:h], top, ((1,), (1,)))
    return jnp.concatenate([left, dot(value, packed[0:h, :], ((1,), (1,)))], 1)


def second_inverse(core, half, other):
    return pl.pallas_call(
        second_kernel,
        in_specs=[SMEM, VMEM, VMEM],
        out_specs=VMEM,
        out_shape=shape(RANK * 3 // 4, RANK),
        scratch_shapes=[scratch(GRAM, RANK), scratch(RANK, RANK), scratch(RANK, RANK)]
        + [scratch(RANK // 2, RANK // 2)] * 2,
        cost_estimate=cost(10_000_000_000),
        compiler_params=params(),
        name="second_inverse",
    )(core, half, other)


def finish_kernel(core_ref, y_ref, inverse_ref, *rest):
    *part_refs, carried_ref, squares_ref, whole = rest
    core, y = core_ref[0], y_ref[0]
    for k in range(4):
        place = lax.rem(y + 4 - k, 4)
        whole[half_of(4 * core + place, PART), :] = part_refs[k][0:PART, :]
        whole[half_of(4 * (1 - core) + place, PART), :] = part_refs[k][PART : 2 * PART, :]
    carried = times_inverse(whole[...], inverse_ref[...])
    carried_ref[...] = carried
    squares = jnp.sum(carried * carried, axis=0, keepdims=True)
    for k in range(32):
        squares_ref[k] = squares


def finish(core, y, inverse, parts):
    return pl.pallas_call(
        finish_kernel,
        in_specs=[SMEM, SMEM] + [VMEM] * 5,
        out_specs=[VMEM] * 2,
        out_shape=[shape(COLS, RANK), shape(32, 1, RANK)],
        scratch_shapes=[scratch(COLS, RANK)],
        compiler_params=params(),
        name="finish",
    )(core, y, inverse, *parts)


def send_columns(out_hbm, staged, semaphores, give):
    wide = ROWS // 2

    def copy(k):
        place = pl.ds(pl.multiple_of(k * wide, wide), wide)
        return pltpu.make_async_copy(staged.at[k], out_hbm.at[:, place], semaphores.at[k])

    def step(k, _):
        staged[k] = give(pl.ds(pl.multiple_of(k * wide, wide), wide))
        copy(k).start()
        return 0

    lax.fori_loop(0, 2, step, 0)
    for k in range(2):
        copy(k).wait()


def feedback_kernel(
    buffer_ref, product_ref, inverse_ref, carried_ref, out_hbm, left_ref, *rest
):
    left_ref[...] = times_inverse(product_ref[...], inverse_ref[...])
    carried = split(carried_ref[...])

    def give(place):
        change = dot3(carried, split(left_ref[place, :]), ((1,), (1,)))
        return buffer_ref[:, place] - (1.0 - MU) * change

    send_columns(out_hbm, *rest, give)


def feedback(buffer, product, inverse, carried):
    return pl.pallas_call(
        feedback_kernel,
        in_specs=[VMEM] * 4,
        out_specs=[HBM, VMEM],
        out_shape=[shape(COLS, ROWS), shape(ROWS, RANK)],
        input_output_aliases={1: 1},
        scratch_shapes=[scratch(2, COLS, ROWS // 2), pltpu.SemaphoreType.DMA((2,))],
        cost_estimate=cost(4_000_000_000),
        compiler_params=params(),
        name="feedback",
    )(buffer, product, inverse, carried)


def update_kernel(left_ref, carried_ref, squares_ref, out_hbm, *rest):
    squares = squares_ref[0]
    for k in range(1, 32):
        squares = squares + squares_ref[k]
    right = carried_ref[...] * (((D * FF / RANK) ** 0.5) / jnp.sqrt(squares + EPS))
    right = split(right)

    def give(place):
        return dot3(right, split(left_ref[place, :]), ((1,), (1,)))

    send_columns(out_hbm, *rest, give)


def update(left, carried, squares):
    return pl.pallas_call(
        update_kernel,
        in_specs=[VMEM] * 3,
        out_specs=HBM,
        out_shape=shape(COLS, ROWS),
        scratch_shapes=[scratch(2, COLS, ROWS // 2), pltpu.SemaphoreType.DMA((2,))],
        compiler_params=params(),
        name="update",
    )(left, carried, squares)


def fold_kernel(parts, value_ref, out_ref):
    size = out_ref.shape[0] // parts
    total = value_ref[0:size, :]
    for k in range(1, parts):
        total = total + value_ref[k * size : (k + 1) * size, :]
    for k in range(parts):
        out_ref[k * size : (k + 1) * size, :] = total


def sum_by_exchange(value, axis, groups):
    value = lax.all_to_all(value, axis, 0, 0, tiled=True, axis_index_groups=groups)
    value = pl.pallas_call(
        functools.partial(fold_kernel, len(groups[0])),
        in_specs=[VMEM],
        out_specs=VMEM,
        out_shape=shape(*value.shape),
        compiler_params=params(),
        name="fold",
    )(value)
    return lax.all_to_all(value, axis, 0, 0, tiled=True, axis_index_groups=groups)


def sum_over_col(blocks, beside):
    with jax.named_scope("sum_over_col"):
        total = blocks[0]
        for k in (3, 2, 1):
            total = total + lax.ppermute(blocks[k], "col", X_SHIFTS[k - 1])
        total, beside = lax.optimization_barrier((total, beside))
        total = sum_by_exchange(total, "col", Z_GROUPS)
        rest = [lax.ppermute(total, "col", X_SHIFTS[k - 1]) for k in (1, 2, 3)]
        return [total] + rest, beside


def sum_over_row(mine, theirs):
    with jax.named_scope("sum_over_row"):
        half = mine + lax.ppermute(theirs, "row", OTHER_CORE)
        half = sum_by_exchange(half, "row", Y_GROUPS)
        return half, lax.ppermute(half, "row", OTHER_CORE)


def sum_and_invert(core, y, mine, theirs):
    with jax.named_scope("sum_and_invert"):
        half = mine + lax.ppermute(theirs, "row", OTHER_CORE)
        gram, half = half[: GRAM // 2], half[GRAM // 2 :]

        def share(k):
            part = lax.dynamic_slice_in_dim(half, (y[0] + k) % 4 * PART, PART)
            return jnp.concatenate([gram, part], 0)

        total = share(0)
        for k in (1, 2, 3):
            total = total + lax.ppermute(share(k), "row", Y_SHIFTS[k - 1])
        other = lax.ppermute(total, "row", OTHER_CORE)
        inverse = second_inverse(core, total, other)
        part = jnp.concatenate([total[GRAM // 2 :], other[GRAM // 2 :]], 0)
        parts = [part] + [lax.ppermute(part, "row", shift) for shift in Y_SHIFTS]
        return inverse, *finish(core, y, inverse, parts)


def on_device(momentum, gradient, right_factor):
    x = lax.axis_index("col")[None] % 4
    core = lax.axis_index("row")[None] % 2
    y = lax.axis_index("row")[None] // 2
    buffer = momentum.T + gradient.T
    left, buffer = sum_over_col(start(x, buffer, right_factor), buffer)
    half, other = sum_over_row(*backward(x, core, buffer, left))
    *blocks, gram = forward(x, core, buffer, half, other)
    product, inverse = sum_over_col(blocks, first_inverse(gram))
    old = prepare(x, inverse, left)
    mine, theirs, product = solve(x, core, buffer, inverse, old, product)
    inverse, carried, squares = sum_and_invert(core, y, mine, theirs)
    squares = lax.all_to_all(squares, "col", 0, 0, tiled=True)
    momentum_next, left = feedback(buffer, product, inverse, carried)
    return (momentum_next.T, update(left, carried, squares).T)


def solution(mesh):
    return jax.shard_map(
        on_device,
        mesh=mesh,
        in_specs=(P("row", "col"), P("row", "col"), P("col", None)),
        out_specs=(P("row", "col"), P("row", "col")),
        check_vma=False,
    )
```

time: 896 us -> 208 us (0.23)
  waiting for transfers between devices: 548 us -> 59.7 us
  other arithmetic: 118 us -> 3.89 us
  blocking collectives: 150 us -> 82.2 us
  matrix products: 40.5 us -> 0 us
  Pallas kernels: 0 us -> 32.9 us
  starting transfers between devices: 0.92 us -> 26.6 us
  between operations: 17.4 us -> 1.05 us
  local copies, waits for them, and re-layouts: 14.8 us -> 0.68 us
    psum x6 -> x0, waiting for transfers between devices: 547 us -> none  [the longest x2 298 us: on_device(): left = lax.psum(partial_value, 'col')]
    psum x2 -> x0, blocking collectives: 150 us -> none  [on_device(): squares = lax.psum(jnp.sum(carried * carried, axis=0), 'col')]
    another operation x18 -> x0, other arithmetic: 111 us -> none  [the longest x13 69.2 us: solve_left(): lower = jnp.linalg.cholesky(gram)]
    all_to_all x0 -> x6, blocking collectives: none -> 82.2 us  [sum_by_exchange(): lax.all_to_all(value, axis, 0, 0, tiled=True, axis_index_groups=groups)]
    ppermute x0 -> x22, waiting for transfers between devices: none -> 53.4 us  [the longest x6 19.1 us: sum_over_col(): rest = [lax.ppermute(total, 'col', X_SHIFTS[k - 1]) for k in (1, 2, 3)]]
    pallas_call x0 -> x13, Pallas kernels: none -> 32.9 us  [the longest x1 8.57 us: second_inverse(): pl.pallas_call(second_kernel, in_specs=[SMEM, VMEM, VMEM], out_specs=VMEM...]
    dot_general x8 -> x0, matrix products: 29.8 us -> none  [the longest x2 9.86 us: on_device(): partial_value = jnp.dot(buffer, right, precision=lax.Precision.HIGHEST)]
    ppermute x0 -> x22, starting transfers between devices: none -> 21.7 us  [the longest x6 6.82 us: sum_over_col(): total = total + lax.ppermute(blocks[k], 'col', X_SHIFTS[k - 1])]
  transfers between devices with their start and end apart: 6 -> 23, of which waited for: 6 -> 18; matrix products, arithmetic and copies ran while one was open for 0% -> 0% of each run, Pallas kernels for 0% -> 10%
where the time goes in v2:
time: 208 us; the launch traced here: 207 us
  blocking collectives  82.2 us (40%)
  waiting for transfers between devices  59.7 us (29%)
  Pallas kernels  32.9 us (16%)
  starting transfers between devices  26.6 us (13%)
  other arithmetic  3.89 us (2%)
    all_to_all x6, blocking collectives, sum_by_exchange(): lax.all_to_all(value, axis, 0, 0, tiled=True, axis_index_groups=groups)  82.2 us
    ppermute x6, waiting for transfers between devices, sum_over_col(): rest = [lax.ppermute(total, 'col', X_SHIFTS[k - 1]) for k in (1, 2, 3)]  19.1 us
    ppermute x6, waiting for transfers between devices, sum_over_col(): total = total + lax.ppermute(blocks[k], 'col', X_SHIFTS[k - 1])  18.9 us
    ppermute x3, waiting for transfers between devices, sum_and_invert(): total = total + lax.ppermute(share(k), 'row', Y_SHIFTS[k - 1])  8.65 us
    pallas_call x1, Pallas kernels, second_inverse(): pl.pallas_call(second_kernel, in_specs=[SMEM, VMEM, VMEM], out_specs=VMEM...  8.57 us
    pallas_call x1, Pallas kernels, first_inverse(): pl.pallas_call(cholesky_inverse, in_specs=[VMEM], out_specs=VMEM, out_sha...  8.4 us
    ppermute x6, starting transfers between devices, sum_over_col(): total = total + lax.ppermute(blocks[k], 'col', X_SHIFTS[k - 1])  6.82 us
    all_to_all x1, waiting for transfers between devices, on_device(): squares = lax.all_to_all(squares, 'col', 0, 0, tiled=True)  6.31 us
  transfers between devices with their start and end apart: 23, of which 18 were waited for; matrix products, arithmetic and copies ran while one was open for 0% of the time, Pallas kernels for 10%

profile of v2, /device:TPU:8, one launch (start us, length us, event | category | flops | bytes accessed | tf_op | source)
XLA Modules:
  0.0 207.1 jit_solution(8834417979915931930)
XLA Ops:
  0.7 2.6 %add_bitcast_fusion.buffer_ref = f32[448,1024]{1,0:T(8,128)S(1)} fusion(f32[1024,448]{0,1:T(8,128)} %param.3, f32[1024,448]{0,1:T(8,128)} %param.4), kind=kLoop, calls=%fused_computation | loop fusion | flops 458752 | bytes 5505024 | tf_op jit(solution)/shard_map/add | solution.py:494
  3.2 1.0 start.1
  4.3 2.8 %collective-permute-start = (f32[256,256]{1,0:T(8,128)S(1)}, f32[256,256]{1,0:T(8,128)S(1)}, u32[]{:S(2)}, u32[]{:S(2)}) collective-permute-start(f32[256,256]{1,0:T(8,128)S(1)} %get-tuple-element.25), channel_id=1, source_target_pairs={{0,3},{1,0},{2,1},{3,2},{4,7},{5,4},{6,5},{7,6},{8,11},{9,8},{10,9... | collective-permute-start | bytes 786440 | tf_op jit(solution)/shard_map/sum_over_col/ppermute | solution.py:457
  7.1 0.8 collective-permute-start.1
  7.9 0.9 collective-permute-start.2
  8.8 9.5 %collective-permute-done = f32[256,256]{1,0:T(8,128)S(1)} collective-permute-done((f32[256,256]{1,0:T(8,128)S(1)}, f32[256,256]{1,0:T(8,128)S(1)}, u32[]{:S(2)}, u32[]{:S(2)}) %collective-permute-start) | collective-permute-done | bytes 262176 | tf_op jit(solution)/shard_map/sum_over_col/ppermute | solution.py:457
  18.3 3.7 %collective-permute-done.2 = f32[256,256]{1,0:T(8,128)S(1)} collective-permute-done((f32[256,256]{1,0:T(8,128)S(1)}, f32[256,256]{1,0:T(8,128)S(1)}, u32[]{:S(2)}, u32[]{:S(2)}) %collective-permute-start.2) | collective-permute-done | bytes 262176 | tf_op jit(solution)/shard_map/sum_over_col/ppermute | solution.py:457
  22.1 20.3 %all_to_all.71 = f32[8,32,256]{2,1,0:T(8,128)S(1)} all-to-all(f32[8,32,256]{2,1,0:T(8,128)S(1)} %bitcast.38), channel_id=1, replica_groups={{0,4,8,12,16,20,24,28},{1,5,9,13,17,21,25,29},{2,6,10,14,18,22,26,30},{..., dimensions={0} | all-to-all | bytes 524288 | tf_op jit(solution)/shard_map/sum_over_col/all_to_all | solution.py:441
  42.4 13.1 %all_to_all.72 = f32[8,32,256]{2,1,0:T(8,128)S(1)} all-to-all(f32[8,32,256]{2,1,0:T(8,128)S(1)} %bitcast.28), channel_id=1, replica_groups={{0,4,8,12,16,20,24,28},{1,5,9,13,17,21,25,29},{2,6,10,14,18,22,26,30},{..., dimensions={0} | all-to-all | bytes 524288 | tf_op jit(solution)/shard_map/sum_over_col/all_to_all | solution.py:450
  55.6 0.8 collective-permute-start.4
  56.4 1.4 collective-permute-start.3
  57.8 5.8 %collective-permute-done.5.rest_3_ = f32[256,256]{1,0:T(8,128)S(1)} collective-permute-done((f32[256,256]{1,0:T(8,128)S(1)}, f32[256,256]{1,0:T(8,128)S(1)}, u32[]{:S(2)}, u32[]{:S(2)}) %collective-permute-start.5) | collective-permute-done | bytes 262176 | tf_op jit(solution)/shard_map/sum_over_col/ppermute | solution.py:460
  63.6 1.6 collective-permute-done.4.rest_2_
  65.2 2.7 %collective-permute-done.3.rest_1_ = f32[256,256]{1,0:T(8,128)S(1)} collective-permute-done((f32[256,256]{1,0:T(8,128)S(1)}, f32[256,256]{1,0:T(8,128)S(1)}, u32[]{:S(2)}, u32[]{:S(2)}) %collective-permute-start.3) | collective-permute-done | bytes 262176 | tf_op jit(solution)/shard_map/sum_over_col/ppermute | solution.py:460
  67.9 1.9 backward.1
  69.9 1.7 collective-permute-done.6
  71.6 11.3 %all_to_all.73 = f32[4,88,256]{2,1,0:T(8,128)S(1)} all-to-all(f32[4,88,256]{2,1,0:T(8,128)S(1)} %bitcast.37), channel_id=1, replica_groups={{0,64,128,192},{32,96,160,224},{1,65,129,193},{33,97,161,225},{2,66,130..., dimensions={0} | all-to-all | bytes 720896 | tf_op jit(solution)/shard_map/sum_over_row/all_to_all | solution.py:441
  82.9 9.6 %all_to_all.74 = f32[4,88,256]{2,1,0:T(8,128)S(1)} all-to-all(f32[4,88,256]{2,1,0:T(8,128)S(1)} %bitcast.22), channel_id=1, replica_groups={{0,64,128,192},{32,96,160,224},{1,65,129,193},{33,97,161,225},{2,66,130..., dimensions={0} | all-to-all | bytes 720896 | tf_op jit(solution)/shard_map/sum_over_row/all_to_all | solution.py:450
  92.5 1.7 collective-permute-done.7.other_ref
  94.2 1.1 forward.1
  95.3 1.3 collective-permute-start.8
  97.6 8.4 %first_inverse.1.inverse_ref = f32[256,256]{1,0:T(8,128)S(1)} custom-call(f32[256,256]{1,0:T(8,128)S(1)} %get-tuple-element.36.gram_ref), custom_call_target="tpu_custom_call" | custom-call | flops 10000000000 | bytes 1000000 | tf_op jit(solution)/shard_map/first_inverse/pallas_call | solution.py:290
  106.0 1.3 collective-permute-done.9
  107.3 4.5 %collective-permute-done.10 = f32[256,256]{1,0:T(8,128)S(1)} collective-permute-done((f32[256,256]{1,0:T(8,128)S(1)}, f32[256,256]{1,0:T(8,128)S(1)}, u32[]{:S(2)}, u32[]{:S(2)}) %collective-permute-start.10) | collective-permute-done | bytes 262176 | tf_op jit(solution)/shard_map/sum_over_col/ppermute | solution.py:457
  111.8 14.7 %all_to_all.75 = f32[8,32,256]{2,1,0:T(8,128)S(1)} all-to-all(f32[8,32,256]{2,1,0:T(8,128)S(1)} %bitcast.39), channel_id=1, replica_groups={{0,4,8,12,16,20,24,28},{1,5,9,13,17,21,25,29},{2,6,10,14,18,22,26,30},{..., dimensions={0} | all-to-all | bytes 524288 | tf_op jit(solution)/shard_map/sum_over_col/all_to_all | solution.py:441
  126.5 13.2 %all_to_all.76 = f32[8,32,256]{2,1,0:T(8,128)S(1)} all-to-all(f32[8,32,256]{2,1,0:T(8,128)S(1)} %bitcast.30), channel_id=1, replica_groups={{0,4,8,12,16,20,24,28},{1,5,9,13,17,21,25,29},{2,6,10,14,18,22,26,30},{..., dimensions={0} | all-to-all | bytes 524288 | tf_op jit(solution)/shard_map/sum_over_col/all_to_all | solution.py:450
  139.8 1.2 collective-permute-start.12
  141.0 1.4 collective-permute-start.11
  143.0 4.7 %collective-permute-done.13.rest_3_ = f32[256,256]{1,0:T(8,128)S(1)} collective-permute-done((f32[256,256]{1,0:T(8,128)S(1)}, f32[256,256]{1,0:T(8,128)S(1)}, u32[]{:S(2)}, u32[]{:S(2)}) %collective-permute-start.13) | collective-permute-done | bytes 262176 | tf_op jit(solution)/shard_map/sum_over_col/ppermute | solution.py:460
  147.7 1.6 collective-permute-done.12.rest_2_
  149.3 2.7 %collective-permute-done.11.rest_1_ = f32[256,256]{1,0:T(8,128)S(1)} collective-permute-done((f32[256,256]{1,0:T(8,128)S(1)}, f32[256,256]{1,0:T(8,128)S(1)}, u32[]{:S(2)}, u32[]{:S(2)}) %collective-permute-start.11) | collective-permute-done | bytes 262176 | tf_op jit(solution)/shard_map/sum_over_col/ppermute | solution.py:460
  152.0 3.9 %solve.1 = (f32[360,256]{1,0:T(8,128)S(1)}, f32[360,256]{1,0:T(8,128)}, f32[1024,256]{1,0:T(8,128)S(1)}) custom-call(s32[1]{0:T(128)S(6)} %select_n.46.x_ref, s32[1]{0:T(128)S(6)} %select_n.47.core_ref, f32[448,1024]{1,0:T(8,128)S(1)} %add_bitcast_fusion.buffer_ref, f32[256,256]{1,0:T(8,128)S(1)} %first_inverse.1.inverse_ref, ...), custom_call_target="tpu_custom_call" | custom-call | tf_op jit(solution)/shard_map/solve/pallas_call | solution.py:255
  155.9 2.0 collective-permute-done.14
  157.9 1.0 add.94
  159.5 3.2 %collective-permute-start.16 = (f32[192,256]{1,0:T(8,128)S(1)}, f32[192,256]{1,0:T(8,128)S(1)}, u32[]{:S(2)}, u32[]{:S(2)}) collective-permute-start(f32[192,256]{1,0:T(8,128)S(1)} %get-tuple-element.51), channel_id=1, source_target_pairs={{0,128},{32,160},{64,192},{96,224},{128,0},{160,32},{192,64},{224,... | collective-permute-start | bytes 589832 | tf_op jit(solution)/shard_map/sum_and_invert/ppermute | solution.py:482
  163.3 3.6 %collective-permute-done.15 = f32[192,256]{1,0:T(8,128)S(1)} collective-permute-done((f32[192,256]{1,0:T(8,128)S(1)}, f32[192,256]{1,0:T(8,128)S(1)}, u32[]{:S(2)}, u32[]{:S(2)}) %collective-permute-start.15) | collective-permute-done | bytes 196640 | tf_op jit(solution)/shard_map/sum_and_invert/ppermute | solution.py:482
  166.9 1.9 collective-permute-done.16
  168.8 3.1 %collective-permute-done.17 = f32[192,256]{1,0:T(8,128)S(1)} collective-permute-done((f32[192,256]{1,0:T(8,128)S(1)}, f32[192,256]{1,0:T(8,128)S(1)}, u32[]{:S(2)}, u32[]{:S(2)}) %collective-permute-start.17) | collective-permute-done | bytes 196640 | tf_op jit(solution)/shard_map/sum_and_invert/ppermute | solution.py:482
  172.1 1.4 collective-permute-done.18.other_ref
  173.6 1.8 collective-permute-start.21
  175.3 1.4 collective-permute-start.20
  176.7 2.5 %collective-permute-start.19 = (f32[112,256]{1,0:T(8,128)S(1)}, f32[112,256]{1,0:T(8,128)S(1)}, u32[]{:S(2)}, u32[]{:S(2)}) collective-permute-start(f32[112,256]{1,0:T(8,128)S(1)} %pad_maximum_fusion.4.rest_0_), channel_id=1, source_target_pairs={{0,64},{32,96},{64,128},{96,160},{128,192},{160,224},{192,0},{224,... | collective-permute-start | bytes 344072 | tf_op jit(solution)/shard_map/sum_and_invert/ppermute | solution.py:486
  179.2 8.6 %second_inverse.1.inverse_ref = f32[192,256]{1,0:T(8,128)S(1)} custom-call(s32[1]{0:T(128)S(6)} %select_n.47.core_ref, f32[192,256]{1,0:T(8,128)S(1)} %fusion.2.half_ref, f32[192,256]{1,0:T(8,128)S(1)} %collective-permute-done.18.other_ref), custom_call_target="tpu_custom_call" | custom-call | flops 10000000000 | bytes 1000000 | tf_op jit(solution)/shard_map/sum_and_invert/second_inverse/pallas_call | solution.py:323
  187.8 0.8 finish.1
  189.2 4.9 %all-to-all-start.6 = ((f32[32,1,256]{2,1,0:T(1,128)}), f32[32,1,256]{2,1,0:T(1,128)}, u32[]{:S(2)}, u32[]{:S(2)}) async-start(f32[32,1,256]{2,1,0:T(1,128)} %copy-done.1), calls=%async_computation.6 | async-start | bytes 65536 | tf_op jit(solution)/shard_map/all_to_all | solution.py:502
  194.2 3.5 %feedback.1 = (f32[448,1024]{1,0:T(8,128)}, f32[1024,256]{1,0:T(8,128)S(1)}) custom-call(f32[448,1024]{1,0:T(8,128)S(1)} %add_bitcast_fusion.buffer_ref, f32[1024,256]{1,0:T(8,128)S(1)} %get-tuple-element.39.product_ref, f32[192,256]{1,0:T(8,128)S(1)} %second_inverse.1.inverse_ref, ...), custom_call_target="tpu_custom_call", output_to_operand_aliasing={{1}: (1, {})} | custom-call | flops 4000000000 | bytes 1000000 | tf_op jit(solution)/shard_map/feedback/pallas_call | solution.py:393
  197.7 6.3 %all-to-all-done.6.squares_ref = f32[32,1,256]{2,1,0:T(1,128)} async-done(((f32[32,1,256]{2,1,0:T(1,128)}), f32[32,1,256]{2,1,0:T(1,128)}, u32[]{:S(2)}, u32[]{:S(2)}) %all-to-all-start.6) | async-done | bytes 32800 | tf_op jit(solution)/shard_map/all_to_all | solution.py:502
  204.0 3.0 %update.1 = f32[448,1024]{1,0:T(8,128)} custom-call(f32[1024,256]{1,0:T(8,128)S(1)} %get-tuple-element.44.left_ref, f32[448,256]{1,0:T(8,128)S(1)} %get-tuple-element.42.carried_ref, f32[32,1,256]{2,1,0:T(1,128)} %all-to-all-done.6.squares_ref), custom_call_target="tpu_custom_call" | custom-call | tf_op jit(solution)/shard_map/update/pallas_call | solution.py:420
  (34 shorter events, 3.9 us)
Async XLA Ops:
  0.6 2.6 %copy-start = (f32[448,256]{1,0:T(8,128)S(1)}, f32[448,256]{1,0:T(8,128)}, u32[]{:S(2)}) copy-start(f32[448,256]{1,0:T(8,128)} %right_ref.1) | copy-start | bytes 1376260
  4.3 14.1 %collective-permute-start = (f32[256,256]{1,0:T(8,128)S(1)}, f32[256,256]{1,0:T(8,128)S(1)}, u32[]{:S(2)}, u32[]{:S(2)}) collective-permute-start(f32[256,256]{1,0:T(8,128)S(1)} %get-tuple-element.25), channel_id=1, source_target_pairs={{0,3},{1,0},{2,1},{3,2},{4,7},{5,4},{6,5},{7,6},{8,11},{9,8},{10,9... | collective-permute-start | bytes 786440 | tf_op jit(solution)/shard_map/sum_over_col/ppermute | solution.py:457
  7.1 11.2 %collective-permute-start.1 = (f32[256,256]{1,0:T(8,128)S(1)}, f32[256,256]{1,0:T(8,128)S(1)}, u32[]{:S(2)}, u32[]{:S(2)}) collective-permute-start(f32[256,256]{1,0:T(8,128)S(1)} %get-tuple-element.26), channel_id=1, source_target_pairs={{0,2},{1,3},{2,0},{3,1},{4,6},{5,7},{6,4},{7,5},{8,10},{9,11},{10,... | collective-permute-start | bytes 786440 | tf_op jit(solution)/shard_map/sum_over_col/ppermute | solution.py:457
  7.9 14.1 %collective-permute-start.2 = (f32[256,256]{1,0:T(8,128)S(1)}, f32[256,256]{1,0:T(8,128)S(1)}, u32[]{:S(2)}, u32[]{:S(2)}) collective-permute-start(f32[256,256]{1,0:T(8,128)S(1)} %get-tuple-element.27), channel_id=1, source_target_pairs={{0,1},{1,2},{2,3},{3,0},{4,5},{5,6},{6,7},{7,4},{8,9},{9,10},{10,1... | collective-permute-start | bytes 786440 | tf_op jit(solution)/shard_map/sum_over_col/ppermute | solution.py:457
  55.5 8.0 %collective-permute-start.5 = (f32[256,256]{1,0:T(8,128)S(1)}, f32[256,256]{1,0:T(8,128)S(1)}, u32[]{:S(2)}, u32[]{:S(2)}) collective-permute-start(f32[256,256]{1,0:T(8,128)S(1)} %bitcast.31), channel_id=1, source_target_pairs={{0,3},{1,0},{2,1},{3,2},{4,7},{5,4},{6,5},{7,6},{8,11},{9,8},{10,9... | collective-permute-start | bytes 786440 | tf_op jit(solution)/shard_map/sum_over_col/ppermute | solution.py:460
  55.6 9.6 %collective-permute-start.4 = (f32[256,256]{1,0:T(8,128)S(1)}, f32[256,256]{1,0:T(8,128)S(1)}, u32[]{:S(2)}, u32[]{:S(2)}) collective-permute-start(f32[256,256]{1,0:T(8,128)S(1)} %bitcast.32), channel_id=1, source_target_pairs={{0,2},{1,3},{2,0},{3,1},{4,6},{5,7},{6,4},{7,5},{8,10},{9,11},{10,... | collective-permute-start | bytes 786440 | tf_op jit(solution)/shard_map/sum_over_col/ppermute | solution.py:460
  56.4 11.5 %collective-permute-start.3 = (f32[256,256]{1,0:T(8,128)S(1)}, f32[256,256]{1,0:T(8,128)S(1)}, u32[]{:S(2)}, u32[]{:S(2)}) collective-permute-start(f32[256,256]{1,0:T(8,128)S(1)} %bitcast.33), channel_id=1, source_target_pairs={{0,1},{1,2},{2,3},{3,0},{4,5},{5,6},{6,7},{7,4},{8,9},{9,10},{10,1... | collective-permute-start | bytes 786440 | tf_op jit(solution)/shard_map/sum_over_col/ppermute | solution.py:460
  69.8 1.8 collective-permute-start.6
  92.5 1.7 collective-permute-start.7
  95.3 10.7 %collective-permute-start.8 = (f32[256,256]{1,0:T(8,128)S(1)}, f32[256,256]{1,0:T(8,128)S(1)}, u32[]{:S(2)}, u32[]{:S(2)}) collective-permute-start(f32[256,256]{1,0:T(8,128)S(1)} %get-tuple-element.33), channel_id=1, source_target_pairs={{0,3},{1,0},{2,1},{3,2},{4,7},{5,4},{6,5},{7,6},{8,11},{9,8},{10,9... | collective-permute-start | bytes 786440 | tf_op jit(solution)/shard_map/sum_over_col/ppermute | solution.py:457
  96.6 10.7 %collective-permute-start.9 = (f32[256,256]{1,0:T(8,128)S(1)}, f32[256,256]{1,0:T(8,128)S(1)}, u32[]{:S(2)}, u32[]{:S(2)}) collective-permute-start(f32[256,256]{1,0:T(8,128)S(1)} %get-tuple-element.34), channel_id=1, source_target_pairs={{0,2},{1,3},{2,0},{3,1},{4,6},{5,7},{6,4},{7,5},{8,10},{9,11},{10,... | collective-permute-start | bytes 786440 | tf_op jit(solution)/shard_map/sum_over_col/ppermute | solution.py:457
  96.8 14.9 %collective-permute-start.10 = (f32[256,256]{1,0:T(8,128)S(1)}, f32[256,256]{1,0:T(8,128)S(1)}, u32[]{:S(2)}, u32[]{:S(2)}) collective-permute-start(f32[256,256]{1,0:T(8,128)S(1)} %get-tuple-element.35), channel_id=1, source_target_pairs={{0,1},{1,2},{2,3},{3,0},{4,5},{5,6},{6,7},{7,4},{8,9},{9,10},{10,1... | collective-permute-start | bytes 786440 | tf_op jit(solution)/shard_map/sum_over_col/ppermute | solution.py:457
  139.8 7.9 %collective-permute-start.13 = (f32[256,256]{1,0:T(8,128)S(1)}, f32[256,256]{1,0:T(8,128)S(1)}, u32[]{:S(2)}, u32[]{:S(2)}) collective-permute-start(f32[256,256]{1,0:T(8,128)S(1)} %bitcast.23), channel_id=1, source_target_pairs={{0,3},{1,0},{2,1},{3,2},{4,7},{5,4},{6,5},{7,6},{8,11},{9,8},{10,9... | collective-permute-start | bytes 786440 | tf_op jit(solution)/shard_map/sum_over_col/ppermute | solution.py:460
  139.8 9.5 %collective-permute-start.12 = (f32[256,256]{1,0:T(8,128)S(1)}, f32[256,256]{1,0:T(8,128)S(1)}, u32[]{:S(2)}, u32[]{:S(2)}) collective-permute-start(f32[256,256]{1,0:T(8,128)S(1)} %bitcast.24), channel_id=1, source_target_pairs={{0,2},{1,3},{2,0},{3,1},{4,6},{5,7},{6,4},{7,5},{8,10},{9,11},{10,... | collective-permute-start | bytes 786440 | tf_op jit(solution)/shard_map/sum_over_col/ppermute | solution.py:460
  141.0 11.0 %collective-permute-start.11 = (f32[256,256]{1,0:T(8,128)S(1)}, f32[256,256]{1,0:T(8,128)S(1)}, u32[]{:S(2)}, u32[]{:S(2)}) collective-permute-start(f32[256,256]{1,0:T(8,128)S(1)} %bitcast.25), channel_id=1, source_target_pairs={{0,1},{1,2},{2,3},{3,0},{4,5},{5,6},{6,7},{7,4},{8,9},{9,10},{10,1... | collective-permute-start | bytes 786440 | tf_op jit(solution)/shard_map/sum_over_col/ppermute | solution.py:460
  155.9 2.0 collective-permute-start.14
  159.1 7.8 %collective-permute-start.15 = (f32[192,256]{1,0:T(8,128)S(1)}, f32[192,256]{1,0:T(8,128)S(1)}, u32[]{:S(2)}, u32[]{:S(2)}) collective-permute-start(f32[192,256]{1,0:T(8,128)S(1)} %get-tuple-element.50), channel_id=1, source_target_pairs={{0,64},{32,96},{64,128},{96,160},{128,192},{160,224},{192,0},{224,... | collective-permute-start | bytes 589832 | tf_op jit(solution)/shard_map/sum_and_invert/ppermute | solution.py:482
  159.5 9.3 %collective-permute-start.16 = (f32[192,256]{1,0:T(8,128)S(1)}, f32[192,256]{1,0:T(8,128)S(1)}, u32[]{:S(2)}, u32[]{:S(2)}) collective-permute-start(f32[192,256]{1,0:T(8,128)S(1)} %get-tuple-element.51), channel_id=1, source_target_pairs={{0,128},{32,160},{64,192},{96,224},{128,0},{160,32},{192,64},{224,... | collective-permute-start | bytes 589832 | tf_op jit(solution)/shard_map/sum_and_invert/ppermute | solution.py:482
  162.7 9.2 %collective-permute-start.17 = (f32[192,256]{1,0:T(8,128)S(1)}, f32[192,256]{1,0:T(8,128)S(1)}, u32[]{:S(2)}, u32[]{:S(2)}) collective-permute-start(f32[192,256]{1,0:T(8,128)S(1)} %get-tuple-element.52), channel_id=1, source_target_pairs={{0,192},{32,224},{64,0},{96,32},{128,64},{160,96},{192,128},{224,1... | collective-permute-start | bytes 589832 | tf_op jit(solution)/shard_map/sum_and_invert/ppermute | solution.py:482
  172.0 1.5 collective-permute-start.18
  173.6 14.2 %collective-permute-start.21 = (f32[112,256]{1,0:T(8,128)S(1)}, f32[112,256]{1,0:T(8,128)S(1)}, u32[]{:S(2)}, u32[]{:S(2)}) collective-permute-start(f32[112,256]{1,0:T(8,128)S(1)} %pad_maximum_fusion.4.rest_0_), channel_id=1, source_target_pairs={{0,192},{32,224},{64,0},{96,32},{128,64},{160,96},{192,128},{224,1... | collective-permute-start | bytes 344072 | tf_op jit(solution)/shard_map/sum_and_invert/ppermute | solution.py:486
  175.3 12.5 %collective-permute-start.20 = (f32[112,256]{1,0:T(8,128)S(1)}, f32[112,256]{1,0:T(8,128)S(1)}, u32[]{:S(2)}, u32[]{:S(2)}) collective-permute-start(f32[112,256]{1,0:T(8,128)S(1)} %pad_maximum_fusion.4.rest_0_), channel_id=1, source_target_pairs={{0,128},{32,160},{64,192},{96,224},{128,0},{160,32},{192,64},{224,... | collective-permute-start | bytes 344072 | tf_op jit(solution)/shard_map/sum_and_invert/ppermute | solution.py:486
  176.7 11.1 %collective-permute-start.19 = (f32[112,256]{1,0:T(8,128)S(1)}, f32[112,256]{1,0:T(8,128)S(1)}, u32[]{:S(2)}, u32[]{:S(2)}) collective-permute-start(f32[112,256]{1,0:T(8,128)S(1)} %pad_maximum_fusion.4.rest_0_), channel_id=1, source_target_pairs={{0,64},{32,96},{64,128},{96,160},{128,192},{160,224},{192,0},{224,... | collective-permute-start | bytes 344072 | tf_op jit(solution)/shard_map/sum_and_invert/ppermute | solution.py:486
  188.6 0.6 copy-start.1
  189.2 14.7 %all-to-all-start.6 = ((f32[32,1,256]{2,1,0:T(1,128)}), f32[32,1,256]{2,1,0:T(1,128)}, u32[]{:S(2)}, u32[]{:S(2)}) async-start(f32[32,1,256]{2,1,0:T(1,128)} %copy-done.1), calls=%async_computation.6 | async-start | bytes 65536 | tf_op jit(solution)/shard_map/all_to_all | solution.py:502

commit v3 on v2

--- a/solution.py
+++ b/solution.py
@@ -35,6 +35,10 @@
 
 def shape(*dims):
     return jax.ShapeDtypeStruct(dims, jnp.float32)
+
+
+def half_shape(*dims):
+    return jax.ShapeDtypeStruct(dims, jnp.bfloat16)
 
 
 def scratch(*dims):
@@ -299,24 +303,20 @@
     )(gram)
 
 
-def second_kernel(core_ref, half_ref, other_ref, out_ref, whole, gram, inverse, block, corner):
+def times_inverse(value, inverse):
+    h = RANK // 2
+    left = dot(value[:, 0:h], inverse[0:h, 0:h], ((1,), (1,)))
+    return jnp.concatenate([left, dot(value, inverse[h:, :], ((1,), (1,)))], 1)
+
+
+def second_kernel(core_ref, half_ref, other_ref, out_ref, whole, gram, block, corner):
     core = core_ref[0]
     whole[half_of(core, GRAM // 2), :] = half_ref[0 : GRAM // 2, :]
     whole[half_of(1 - core, GRAM // 2), :] = other_ref[0 : GRAM // 2, :]
     scale = 1.0 / jnp.sqrt(jnp.maximum(whole[RANK : RANK + 1, :], 0.0) + EPS)
     gram[...] = (whole[0:RANK, :] * scale).T * scale
-    cholesky_inverse(gram, inverse, block, corner)
-    h, q = RANK // 2, RANK // 4
-    out_ref[0:h, :] = inverse[h:, :] * scale
-    out_ref[h:, 0:h] = inverse[0:q, 0:h] * scale[:, 0:h]
-    out_ref[h:, h:] = inverse[q:h, 0:h] * scale[:, 0:h]
-
-
-def times_inverse(value, packed):
-    h = RANK // 2
-    top = jnp.concatenate([packed[h:, 0:h], packed[h:, h:]], 0)
-    left = dot(value[:, 0:h], top, ((1,), (1,)))
-    return jnp.concatenate([left, dot(value, packed[0:h, :], ((1,), (1,)))], 1)
+    cholesky_inverse(gram, out_ref, block, corner)
+    out_ref[...] = out_ref[...] * scale
 
 
 def second_inverse(core, half, other):
@@ -324,8 +324,8 @@
         second_kernel,
         in_specs=[SMEM, VMEM, VMEM],
         out_specs=VMEM,
-        out_shape=shape(RANK * 3 // 4, RANK),
-        scratch_shapes=[scratch(GRAM, RANK), scratch(RANK, RANK), scratch(RANK, RANK)]
+        out_shape=shape(RANK, RANK),
+        scratch_shapes=[scratch(GRAM, RANK), scratch(RANK, RANK)]
         + [scratch(RANK // 2, RANK // 2)] * 2,
         cost_estimate=cost(10_000_000_000),
         compiler_params=params(),
@@ -377,13 +377,14 @@
 
 
 def feedback_kernel(
-    buffer_ref, product_ref, inverse_ref, carried_ref, out_hbm, left_ref, *rest
+    buffer_ref, product_ref, inverse_ref, carried_ref, out_hbm, high_ref, low_ref, *rest
 ):
-    left_ref[...] = times_inverse(product_ref[...], inverse_ref[...])
+    left = times_inverse(product_ref[...], inverse_ref[...])
+    high_ref[...], low_ref[...] = split(left)
     carried = split(carried_ref[...])
 
     def give(place):
-        change = dot3(carried, split(left_ref[place, :]), ((1,), (1,)))
+        change = dot3(carried, (high_ref[place, :], low_ref[place, :]), ((1,), (1,)))
         return buffer_ref[:, place] - (1.0 - MU) * change
 
     send_columns(out_hbm, *rest, give)
@@ -393,9 +394,8 @@
     return pl.pallas_call(
         feedback_kernel,
         in_specs=[VMEM] * 4,
-        out_specs=[HBM, VMEM],
-        out_shape=[shape(COLS, ROWS), shape(ROWS, RANK)],
-        input_output_aliases={1: 1},
+        out_specs=[HBM, VMEM, VMEM],
+        out_shape=[shape(COLS, ROWS)] + [half_shape(ROWS, RANK)] * 2,
         scratch_shapes=[scratch(2, COLS, ROWS // 2), pltpu.SemaphoreType.DMA((2,))],
         cost_estimate=cost(4_000_000_000),
         compiler_params=params(),
@@ -403,7 +403,7 @@
     )(buffer, product, inverse, carried)
 
 
-def update_kernel(left_ref, carried_ref, squares_ref, out_hbm, *rest):
+def update_kernel(high_ref, low_ref, carried_ref, squares_ref, out_hbm, *rest):
     squares = squares_ref[0]
     for k in range(1, 32):
         squares = squares + squares_ref[k]
@@ -411,21 +411,21 @@
     right = split(right)
 
     def give(place):
-        return dot3(right, split(left_ref[place, :]), ((1,), (1,)))
+        return dot3(right, (high_ref[place, :], low_ref[place, :]), ((1,), (1,)))
 
     send_columns(out_hbm, *rest, give)
 
 
-def update(left, carried, squares):
+def update(high, low, carried, squares):
     return pl.pallas_call(
         update_kernel,
-        in_specs=[VMEM] * 3,
+        in_specs=[VMEM] * 4,
         out_specs=HBM,
         out_shape=shape(COLS, ROWS),
         scratch_shapes=[scratch(2, COLS, ROWS // 2), pltpu.SemaphoreType.DMA((2,))],
         compiler_params=params(),
         name="update",
-    )(left, carried, squares)
+    )(high, low, carried, squares)
 
 
 def fold_kernel(parts, value_ref, out_ref):
@@ -500,8 +500,8 @@
     mine, theirs, product = solve(x, core, buffer, inverse, old, product)
     inverse, carried, squares = sum_and_invert(core, y, mine, theirs)
     squares = lax.all_to_all(squares, "col", 0, 0, tiled=True)
-    momentum_next, left = feedback(buffer, product, inverse, carried)
-    return (momentum_next.T, update(left, carried, squares).T)
+    momentum_next, high, low = feedback(buffer, product, inverse, carried)
+    return (momentum_next.T, update(high, low, carried, squares).T)
 
 
 def solution(mesh):

time: 208 us -> 206 us (level)
  waiting for transfers between devices: 59.7 us -> 57.1 us
  local copies, waits for them, and re-layouts: 0.68 us -> 3.21 us
    unnamed x4 -> x10, local copies, waits for them, and re-layouts: 0.61 us -> 3.14 us
    all_to_all x1, waiting for transfers between devices: 6.31 us -> 4.11 us  [on_device(): squares = lax.all_to_all(squares, 'col', 0, 0, tiled=True)]
where the time goes in v3:
time: 206 us; the launch traced here: 205 us
  blocking collectives  82.2 us (40%)
  waiting for transfers between devices  57.1 us (28%)
  Pallas kernels  32.3 us (16%)
  starting transfers between devices  26.6 us (13%)
  local copies, waits for them, and re-layouts  3.21 us (2%)
  other arithmetic  2.78 us (1%)
    all_to_all x6, blocking collectives, sum_by_exchange(): lax.all_to_all(value, axis, 0, 0, tiled=True, axis_index_groups=groups)  82.2 us
    ppermute x6, waiting for transfers between devices, sum_over_col(): rest = [lax.ppermute(total, 'col', X_SHIFTS[k - 1]) for k in (1, 2, 3)]  19 us
    ppermute x6, waiting for transfers between devices, sum_over_col(): total = total + lax.ppermute(blocks[k], 'col', X_SHIFTS[k - 1])  18.9 us
    ppermute x3, waiting for transfers between devices, sum_and_invert(): total = total + lax.ppermute(share(k), 'row', Y_SHIFTS[k - 1])  8.64 us
    pallas_call x1, Pallas kernels, second_inverse(): pl.pallas_call(second_kernel, in_specs=[SMEM, VMEM, VMEM], out_specs=VMEM...  8.56 us
    pallas_call x1, Pallas kernels, first_inverse(): pl.pallas_call(cholesky_inverse, in_specs=[VMEM], out_specs=VMEM, out_sha...  8.4 us
    ppermute x6, starting transfers between devices, sum_over_col(): total = total + lax.ppermute(blocks[k], 'col', X_SHIFTS[k - 1])  6.82 us
    ppermute x3, starting transfers between devices, sum_and_invert(): parts = [part] + [lax.ppermute(part, 'row', shift) for shift in Y_SHIFTS]  5.67 us
  transfers between devices with their start and end apart: 23, of which 18 were waited for; matrix products, arithmetic and copies ran while one was open for 0% of the time, Pallas kernels for 10%

profile of v3, /device:TPU:8, one launch (start us, length us, event | category | flops | bytes accessed | tf_op | source)
XLA Modules:
  0.0 205.3 jit_solution(847948164063871173)
XLA Ops:
  0.7 2.4 %add_bitcast_fusion.buffer_ref = f32[448,1024]{1,0:T(8,128)S(1)} fusion(f32[1024,448]{0,1:T(8,128)} %param.3, f32[1024,448]{0,1:T(8,128)} %param.4), kind=kLoop, calls=%fused_computation | loop fusion | flops 458752 | bytes 5505024 | tf_op jit(solution)/shard_map/add | solution.py:494
  3.1 1.1 start.1
  4.2 2.8 %collective-permute-start = (f32[256,256]{1,0:T(8,128)S(1)}, f32[256,256]{1,0:T(8,128)S(1)}, u32[]{:S(2)}, u32[]{:S(2)}) collective-permute-start(f32[256,256]{1,0:T(8,128)S(1)} %get-tuple-element.26), channel_id=1, source_target_pairs={{0,3},{1,0},{2,1},{3,2},{4,7},{5,4},{6,5},{7,6},{8,11},{9,8},{10,9... | collective-permute-start | bytes 786440 | tf_op jit(solution)/shard_map/sum_over_col/ppermute | solution.py:457
  7.8 0.9 collective-permute-start.2
  8.7 9.5 %collective-permute-done = f32[256,256]{1,0:T(8,128)S(1)} collective-permute-done((f32[256,256]{1,0:T(8,128)S(1)}, f32[256,256]{1,0:T(8,128)S(1)}, u32[]{:S(2)}, u32[]{:S(2)}) %collective-permute-start) | collective-permute-done | bytes 262176 | tf_op jit(solution)/shard_map/sum_over_col/ppermute | solution.py:457
  18.2 3.7 %collective-permute-done.2 = f32[256,256]{1,0:T(8,128)S(1)} collective-permute-done((f32[256,256]{1,0:T(8,128)S(1)}, f32[256,256]{1,0:T(8,128)S(1)}, u32[]{:S(2)}, u32[]{:S(2)}) %collective-permute-start.2) | collective-permute-done | bytes 262176 | tf_op jit(solution)/shard_map/sum_over_col/ppermute | solution.py:457
  22.0 20.3 %all_to_all.71 = f32[8,32,256]{2,1,0:T(8,128)S(1)} all-to-all(f32[8,32,256]{2,1,0:T(8,128)S(1)} %bitcast.38), channel_id=1, replica_groups={{0,4,8,12,16,20,24,28},{1,5,9,13,17,21,25,29},{2,6,10,14,18,22,26,30},{..., dimensions={0} | all-to-all | bytes 524288 | tf_op jit(solution)/shard_map/sum_over_col/all_to_all | solution.py:441
  42.3 13.1 %all_to_all.72 = f32[8,32,256]{2,1,0:T(8,128)S(1)} all-to-all(f32[8,32,256]{2,1,0:T(8,128)S(1)} %bitcast.28), channel_id=1, replica_groups={{0,4,8,12,16,20,24,28},{1,5,9,13,17,21,25,29},{2,6,10,14,18,22,26,30},{..., dimensions={0} | all-to-all | bytes 524288 | tf_op jit(solution)/shard_map/sum_over_col/all_to_all | solution.py:450
  56.2 1.4 collective-permute-start.3
  57.7 5.8 %collective-permute-done.5.rest_3_ = f32[256,256]{1,0:T(8,128)S(1)} collective-permute-done((f32[256,256]{1,0:T(8,128)S(1)}, f32[256,256]{1,0:T(8,128)S(1)}, u32[]{:S(2)}, u32[]{:S(2)}) %collective-permute-start.5) | collective-permute-done | bytes 262176 | tf_op jit(solution)/shard_map/sum_over_col/ppermute | solution.py:460
  63.5 1.6 collective-permute-done.4.rest_2_
  65.1 2.7 %collective-permute-done.3.rest_1_ = f32[256,256]{1,0:T(8,128)S(1)} collective-permute-done((f32[256,256]{1,0:T(8,128)S(1)}, f32[256,256]{1,0:T(8,128)S(1)}, u32[]{:S(2)}, u32[]{:S(2)}) %collective-permute-start.3) | collective-permute-done | bytes 262176 | tf_op jit(solution)/shard_map/sum_over_col/ppermute | solution.py:460
  67.7 1.9 backward.1
  69.8 1.7 collective-permute-done.6
  71.5 11.3 %all_to_all.73 = f32[4,88,256]{2,1,0:T(8,128)S(1)} all-to-all(f32[4,88,256]{2,1,0:T(8,128)S(1)} %bitcast.37), channel_id=1, replica_groups={{0,64,128,192},{32,96,160,224},{1,65,129,193},{33,97,161,225},{2,66,130..., dimensions={0} | all-to-all | bytes 720896 | tf_op jit(solution)/shard_map/sum_over_row/all_to_all | solution.py:441
  82.8 9.6 %all_to_all.74 = f32[4,88,256]{2,1,0:T(8,128)S(1)} all-to-all(f32[4,88,256]{2,1,0:T(8,128)S(1)} %bitcast.22), channel_id=1, replica_groups={{0,64,128,192},{32,96,160,224},{1,65,129,193},{33,97,161,225},{2,66,130..., dimensions={0} | all-to-all | bytes 720896 | tf_op jit(solution)/shard_map/sum_over_row/all_to_all | solution.py:450
  92.4 1.7 collective-permute-done.7.other_ref
  94.1 1.1 forward.1
  95.2 1.3 collective-permute-start.8
  97.5 8.4 %first_inverse.1.inverse_ref = f32[256,256]{1,0:T(8,128)S(1)} custom-call(f32[256,256]{1,0:T(8,128)S(1)} %get-tuple-element.37.gram_ref), custom_call_target="tpu_custom_call" | custom-call | flops 10000000000 | bytes 1000000 | tf_op jit(solution)/shard_map/first_inverse/pallas_call | solution.py:294
  105.9 1.3 collective-permute-done.9
  107.2 4.4 %collective-permute-done.10 = f32[256,256]{1,0:T(8,128)S(1)} collective-permute-done((f32[256,256]{1,0:T(8,128)S(1)}, f32[256,256]{1,0:T(8,128)S(1)}, u32[]{:S(2)}, u32[]{:S(2)}) %collective-permute-start.10) | collective-permute-done | bytes 262176 | tf_op jit(solution)/shard_map/sum_over_col/ppermute | solution.py:457
  111.7 14.7 %all_to_all.75 = f32[8,32,256]{2,1,0:T(8,128)S(1)} all-to-all(f32[8,32,256]{2,1,0:T(8,128)S(1)} %bitcast.39), channel_id=1, replica_groups={{0,4,8,12,16,20,24,28},{1,5,9,13,17,21,25,29},{2,6,10,14,18,22,26,30},{..., dimensions={0} | all-to-all | bytes 524288 | tf_op jit(solution)/shard_map/sum_over_col/all_to_all | solution.py:441
  126.4 13.2 %all_to_all.76 = f32[8,32,256]{2,1,0:T(8,128)S(1)} all-to-all(f32[8,32,256]{2,1,0:T(8,128)S(1)} %bitcast.30), channel_id=1, replica_groups={{0,4,8,12,16,20,24,28},{1,5,9,13,17,21,25,29},{2,6,10,14,18,22,26,30},{..., dimensions={0} | all-to-all | bytes 524288 | tf_op jit(solution)/shard_map/sum_over_col/all_to_all | solution.py:450
  139.7 1.2 collective-permute-start.12
  140.9 1.4 collective-permute-start.11
  142.9 4.7 %collective-permute-done.13.rest_3_ = f32[256,256]{1,0:T(8,128)S(1)} collective-permute-done((f32[256,256]{1,0:T(8,128)S(1)}, f32[256,256]{1,0:T(8,128)S(1)}, u32[]{:S(2)}, u32[]{:S(2)}) %collective-permute-start.13) | collective-permute-done | bytes 262176 | tf_op jit(solution)/shard_map/sum_over_col/ppermute | solution.py:460
  147.6 1.6 collective-permute-done.12.rest_2_
  149.1 2.7 %collective-permute-done.11.rest_1_ = f32[256,256]{1,0:T(8,128)S(1)} collective-permute-done((f32[256,256]{1,0:T(8,128)S(1)}, f32[256,256]{1,0:T(8,128)S(1)}, u32[]{:S(2)}, u32[]{:S(2)}) %collective-permute-start.11) | collective-permute-done | bytes 262176 | tf_op jit(solution)/shard_map/sum_over_col/ppermute | solution.py:460
  151.9 3.4 %solve.1 = (f32[360,256]{1,0:T(8,128)S(1)}, f32[360,256]{1,0:T(8,128)S(1)}, f32[1024,256]{1,0:T(8,128)S(1)}) custom-call(s32[1]{0:T(128)S(6)} %select_n.46.x_ref, s32[1]{0:T(128)S(6)} %select_n.47.core_ref, f32[448,1024]{1,0:T(8,128)S(1)} %add_bitcast_fusion.buffer_ref, f32[256,256]{1,0:T(8,128)S(1)} %first_inverse.1.inverse_ref, ...), custom_call_target="tpu_custom_call" | custom-call | tf_op jit(solution)/shard_map/solve/pallas_call | solution.py:259
  155.2 1.0 copy-done.3
  156.2 1.7 collective-permute-done.14
  158.5 3.2 %collective-permute-start.16 = (f32[192,256]{1,0:T(8,128)S(1)}, f32[192,256]{1,0:T(8,128)S(1)}, u32[]{:S(2)}, u32[]{:S(2)}) collective-permute-start(f32[192,256]{1,0:T(8,128)S(1)} %get-tuple-element.53), channel_id=1, source_target_pairs={{0,128},{32,160},{64,192},{96,224},{128,0},{160,32},{192,64},{224,... | collective-permute-start | bytes 589832 | tf_op jit(solution)/shard_map/sum_and_invert/ppermute | solution.py:482
  162.3 3.6 %collective-permute-done.15 = f32[192,256]{1,0:T(8,128)S(1)} collective-permute-done((f32[192,256]{1,0:T(8,128)S(1)}, f32[192,256]{1,0:T(8,128)S(1)}, u32[]{:S(2)}, u32[]{:S(2)}) %collective-permute-start.15) | collective-permute-done | bytes 196640 | tf_op jit(solution)/shard_map/sum_and_invert/ppermute | solution.py:482
  165.9 1.9 collective-permute-done.16
  167.8 3.1 %collective-permute-done.17 = f32[192,256]{1,0:T(8,128)S(1)} collective-permute-done((f32[192,256]{1,0:T(8,128)S(1)}, f32[192,256]{1,0:T(8,128)S(1)}, u32[]{:S(2)}, u32[]{:S(2)}) %collective-permute-start.17) | collective-permute-done | bytes 196640 | tf_op jit(solution)/shard_map/sum_and_invert/ppermute | solution.py:482
  171.1 1.4 collective-permute-done.18.other_ref
  172.5 1.8 collective-permute-start.21
  174.3 1.4 collective-permute-start.20
  175.7 2.5 %collective-permute-start.19 = (f32[112,256]{1,0:T(8,128)S(1)}, f32[112,256]{1,0:T(8,128)S(1)}, u32[]{:S(2)}, u32[]{:S(2)}) collective-permute-start(f32[112,256]{1,0:T(8,128)S(1)} %pad_maximum_fusion.4.rest_0_), channel_id=1, source_target_pairs={{0,64},{32,96},{64,128},{96,160},{128,192},{160,224},{192,0},{224,... | collective-permute-start | bytes 344072 | tf_op jit(solution)/shard_map/sum_and_invert/ppermute | solution.py:486
  178.2 8.6 %second_inverse.1.inverse_ref = f32[256,256]{1,0:T(8,128)S(1)} custom-call(s32[1]{0:T(128)S(6)} %select_n.47.core_ref, f32[192,256]{1,0:T(8,128)S(1)} %fusion.2.half_ref, f32[192,256]{1,0:T(8,128)S(1)} %collective-permute-done.18.other_ref), custom_call_target="tpu_custom_call" | custom-call | flops 10000000000 | bytes 1000000 | tf_op jit(solution)/shard_map/sum_and_invert/second_inverse/pallas_call | solution.py:323
  186.8 1.4 finish.1
  188.2 4.8 %all-to-all-start.6 = ((f32[32,1,256]{2,1,0:T(1,128)}), f32[32,1,256]{2,1,0:T(1,128)S(1)}, u32[]{:S(2)}, u32[]{:S(2)}) async-start(f32[32,1,256]{2,1,0:T(1,128)} %get-tuple-element.47), calls=%async_computation.6 | async-start | bytes 65536 | tf_op jit(solution)/shard_map/all_to_all | solution.py:502
  193.1 0.9 copy-done.2
  194.0 1.2 copy-done.4
  195.2 3.5 %feedback.1 = (f32[448,1024]{1,0:T(8,128)}, bf16[1024,256]{1,0:T(8,128)(2,1)S(1)}, bf16[1024,256]{1,0:T(8,128)(2,1)S(1)}) custom-call(f32[448,1024]{1,0:T(8,128)S(1)} %add_bitcast_fusion.buffer_ref, f32[1024,256]{1,0:T(8,128)S(1)} %copy-done.4, f32[256,256]{1,0:T(8,128)S(1)} %copy-done.2, f32[448,256]{1,0:T(8,128)S(1)} %get-tuple-element.43.carried_ref), custom_call_target="tpu_custom_call" | custom-call | flops 4000000000 | bytes 1000000 | tf_op jit(solution)/shard_map/feedback/pallas_call | solution.py:394
  198.8 4.1 %all-to-all-done.6.squares_ref = f32[32,1,256]{2,1,0:T(1,128)S(1)} async-done(((f32[32,1,256]{2,1,0:T(1,128)}), f32[32,1,256]{2,1,0:T(1,128)S(1)}, u32[]{:S(2)}, u32[]{:S(2)}) %all-to-all-start.6) | async-done | bytes 32800 | tf_op jit(solution)/shard_map/all_to_all | solution.py:502
  202.9 2.2 %update.1 = f32[448,1024]{1,0:T(8,128)} custom-call(bf16[1024,256]{1,0:T(8,128)(2,1)S(1)} %get-tuple-element.45.high_ref, bf16[1024,256]{1,0:T(8,128)(2,1)S(1)} %get-tuple-element.46.low_ref, f32[448,256]{1,0:T(8,128)S(1)} %get-tuple-element.43.carried_ref, f32[32,1,256]{2,1,0:T(1,128)S(1)} %all-to-all-done.6.squares_ref), custom_call_target="tpu_custom_call" | custom-call | tf_op jit(solution)/shard_map/update/pallas_call | solution.py:420
  (40 shorter events, 5.0 us)
Async XLA Ops:
  0.6 2.4 %copy-start = (f32[448,256]{1,0:T(8,128)S(1)}, f32[448,256]{1,0:T(8,128)}, u32[]{:S(2)}) copy-start(f32[448,256]{1,0:T(8,128)} %right_ref.1) | copy-start | bytes 1376260
  4.2 14.1 %collective-permute-start = (f32[256,256]{1,0:T(8,128)S(1)}, f32[256,256]{1,0:T(8,128)S(1)}, u32[]{:S(2)}, u32[]{:S(2)}) collective-permute-start(f32[256,256]{1,0:T(8,128)S(1)} %get-tuple-element.26), channel_id=1, source_target_pairs={{0,3},{1,0},{2,1},{3,2},{4,7},{5,4},{6,5},{7,6},{8,11},{9,8},{10,9... | collective-permute-start | bytes 786440 | tf_op jit(solution)/shard_map/sum_over_col/ppermute | solution.py:457
  7.0 11.2 %collective-permute-start.1 = (f32[256,256]{1,0:T(8,128)S(1)}, f32[256,256]{1,0:T(8,128)S(1)}, u32[]{:S(2)}, u32[]{:S(2)}) collective-permute-start(f32[256,256]{1,0:T(8,128)S(1)} %get-tuple-element.27), channel_id=1, source_target_pairs={{0,2},{1,3},{2,0},{3,1},{4,6},{5,7},{6,4},{7,5},{8,10},{9,11},{10,... | collective-permute-start | bytes 786440 | tf_op jit(solution)/shard_map/sum_over_col/ppermute | solution.py:457
  7.8 14.1 %collective-permute-start.2 = (f32[256,256]{1,0:T(8,128)S(1)}, f32[256,256]{1,0:T(8,128)S(1)}, u32[]{:S(2)}, u32[]{:S(2)}) collective-permute-start(f32[256,256]{1,0:T(8,128)S(1)} %get-tuple-element.28), channel_id=1, source_target_pairs={{0,1},{1,2},{2,3},{3,0},{4,5},{5,6},{6,7},{7,4},{8,9},{9,10},{10,1... | collective-permute-start | bytes 786440 | tf_op jit(solution)/shard_map/sum_over_col/ppermute | solution.py:457
  55.4 8.0 %collective-permute-start.5 = (f32[256,256]{1,0:T(8,128)S(1)}, f32[256,256]{1,0:T(8,128)S(1)}, u32[]{:S(2)}, u32[]{:S(2)}) collective-permute-start(f32[256,256]{1,0:T(8,128)S(1)} %bitcast.31), channel_id=1, source_target_pairs={{0,3},{1,0},{2,1},{3,2},{4,7},{5,4},{6,5},{7,6},{8,11},{9,8},{10,9... | collective-permute-start | bytes 786440 | tf_op jit(solution)/shard_map/sum_over_col/ppermute | solution.py:460
  55.4 9.6 %collective-permute-start.4 = (f32[256,256]{1,0:T(8,128)S(1)}, f32[256,256]{1,0:T(8,128)S(1)}, u32[]{:S(2)}, u32[]{:S(2)}) collective-permute-start(f32[256,256]{1,0:T(8,128)S(1)} %bitcast.32), channel_id=1, source_target_pairs={{0,2},{1,3},{2,0},{3,1},{4,6},{5,7},{6,4},{7,5},{8,10},{9,11},{10,... | collective-permute-start | bytes 786440 | tf_op jit(solution)/shard_map/sum_over_col/ppermute | solution.py:460
  56.2 11.5 %collective-permute-start.3 = (f32[256,256]{1,0:T(8,128)S(1)}, f32[256,256]{1,0:T(8,128)S(1)}, u32[]{:S(2)}, u32[]{:S(2)}) collective-permute-start(f32[256,256]{1,0:T(8,128)S(1)} %bitcast.33), channel_id=1, source_target_pairs={{0,1},{1,2},{2,3},{3,0},{4,5},{5,6},{6,7},{7,4},{8,9},{9,10},{10,1... | collective-permute-start | bytes 786440 | tf_op jit(solution)/shard_map/sum_over_col/ppermute | solution.py:460
  69.7 1.8 collective-permute-start.6
  92.4 1.7 collective-permute-start.7
  95.2 10.7 %collective-permute-start.8 = (f32[256,256]{1,0:T(8,128)S(1)}, f32[256,256]{1,0:T(8,128)S(1)}, u32[]{:S(2)}, u32[]{:S(2)}) collective-permute-start(f32[256,256]{1,0:T(8,128)S(1)} %get-tuple-element.34), channel_id=1, source_target_pairs={{0,3},{1,0},{2,1},{3,2},{4,7},{5,4},{6,5},{7,6},{8,11},{9,8},{10,9... | collective-permute-start | bytes 786440 | tf_op jit(solution)/shard_map/sum_over_col/ppermute | solution.py:457
  96.5 10.7 %collective-permute-start.9 = (f32[256,256]{1,0:T(8,128)S(1)}, f32[256,256]{1,0:T(8,128)S(1)}, u32[]{:S(2)}, u32[]{:S(2)}) collective-permute-start(f32[256,256]{1,0:T(8,128)S(1)} %get-tuple-element.35), channel_id=1, source_target_pairs={{0,2},{1,3},{2,0},{3,1},{4,6},{5,7},{6,4},{7,5},{8,10},{9,11},{10,... | collective-permute-start | bytes 786440 | tf_op jit(solution)/shard_map/sum_over_col/ppermute | solution.py:457
  96.7 14.9 %collective-permute-start.10 = (f32[256,256]{1,0:T(8,128)S(1)}, f32[256,256]{1,0:T(8,128)S(1)}, u32[]{:S(2)}, u32[]{:S(2)}) collective-permute-start(f32[256,256]{1,0:T(8,128)S(1)} %get-tuple-element.36), channel_id=1, source_target_pairs={{0,1},{1,2},{2,3},{3,0},{4,5},{5,6},{6,7},{7,4},{8,9},{9,10},{10,1... | collective-permute-start | bytes 786440 | tf_op jit(solution)/shard_map/sum_over_col/ppermute | solution.py:457
  139.7 7.9 %collective-permute-start.13 = (f32[256,256]{1,0:T(8,128)S(1)}, f32[256,256]{1,0:T(8,128)S(1)}, u32[]{:S(2)}, u32[]{:S(2)}) collective-permute-start(f32[256,256]{1,0:T(8,128)S(1)} %bitcast.23), channel_id=1, source_target_pairs={{0,3},{1,0},{2,1},{3,2},{4,7},{5,4},{6,5},{7,6},{8,11},{9,8},{10,9... | collective-permute-start | bytes 786440 | tf_op jit(solution)/shard_map/sum_over_col/ppermute | solution.py:460
  139.7 9.5 %collective-permute-start.12 = (f32[256,256]{1,0:T(8,128)S(1)}, f32[256,256]{1,0:T(8,128)S(1)}, u32[]{:S(2)}, u32[]{:S(2)}) collective-permute-start(f32[256,256]{1,0:T(8,128)S(1)} %bitcast.24), channel_id=1, source_target_pairs={{0,2},{1,3},{2,0},{3,1},{4,6},{5,7},{6,4},{7,5},{8,10},{9,11},{10,... | collective-permute-start | bytes 786440 | tf_op jit(solution)/shard_map/sum_over_col/ppermute | solution.py:460
  140.9 11.0 %collective-permute-start.11 = (f32[256,256]{1,0:T(8,128)S(1)}, f32[256,256]{1,0:T(8,128)S(1)}, u32[]{:S(2)}, u32[]{:S(2)}) collective-permute-start(f32[256,256]{1,0:T(8,128)S(1)} %bitcast.25), channel_id=1, source_target_pairs={{0,1},{1,2},{2,3},{3,0},{4,5},{5,6},{6,7},{7,4},{8,9},{9,10},{10,1... | collective-permute-start | bytes 786440 | tf_op jit(solution)/shard_map/sum_over_col/ppermute | solution.py:460
  155.2 1.0 copy-start.3
  156.2 1.7 collective-permute-start.14
  158.1 7.8 %collective-permute-start.15 = (f32[192,256]{1,0:T(8,128)S(1)}, f32[192,256]{1,0:T(8,128)S(1)}, u32[]{:S(2)}, u32[]{:S(2)}) collective-permute-start(f32[192,256]{1,0:T(8,128)S(1)} %get-tuple-element.52), channel_id=1, source_target_pairs={{0,64},{32,96},{64,128},{96,160},{128,192},{160,224},{192,0},{224,... | collective-permute-start | bytes 589832 | tf_op jit(solution)/shard_map/sum_and_invert/ppermute | solution.py:482
  158.5 9.3 %collective-permute-start.16 = (f32[192,256]{1,0:T(8,128)S(1)}, f32[192,256]{1,0:T(8,128)S(1)}, u32[]{:S(2)}, u32[]{:S(2)}) collective-permute-start(f32[192,256]{1,0:T(8,128)S(1)} %get-tuple-element.53), channel_id=1, source_target_pairs={{0,128},{32,160},{64,192},{96,224},{128,0},{160,32},{192,64},{224,... | collective-permute-start | bytes 589832 | tf_op jit(solution)/shard_map/sum_and_invert/ppermute | solution.py:482
  161.7 9.2 %collective-permute-start.17 = (f32[192,256]{1,0:T(8,128)S(1)}, f32[192,256]{1,0:T(8,128)S(1)}, u32[]{:S(2)}, u32[]{:S(2)}) collective-permute-start(f32[192,256]{1,0:T(8,128)S(1)} %get-tuple-element.54), channel_id=1, source_target_pairs={{0,192},{32,224},{64,0},{96,32},{128,64},{160,96},{192,128},{224,1... | collective-permute-start | bytes 589832 | tf_op jit(solution)/shard_map/sum_and_invert/ppermute | solution.py:482
  171.0 1.5 collective-permute-start.18
  172.5 14.3 %collective-permute-start.21 = (f32[112,256]{1,0:T(8,128)S(1)}, f32[112,256]{1,0:T(8,128)S(1)}, u32[]{:S(2)}, u32[]{:S(2)}) collective-permute-start(f32[112,256]{1,0:T(8,128)S(1)} %pad_maximum_fusion.4.rest_0_), channel_id=1, source_target_pairs={{0,192},{32,224},{64,0},{96,32},{128,64},{160,96},{192,128},{224,1... | collective-permute-start | bytes 344072 | tf_op jit(solution)/shard_map/sum_and_invert/ppermute | solution.py:486
  174.3 12.5 %collective-permute-start.20 = (f32[112,256]{1,0:T(8,128)S(1)}, f32[112,256]{1,0:T(8,128)S(1)}, u32[]{:S(2)}, u32[]{:S(2)}) collective-permute-start(f32[112,256]{1,0:T(8,128)S(1)} %pad_maximum_fusion.4.rest_0_), channel_id=1, source_target_pairs={{0,128},{32,160},{64,192},{96,224},{128,0},{160,32},{192,64},{224,... | collective-permute-start | bytes 344072 | tf_op jit(solution)/shard_map/sum_and_invert/ppermute | solution.py:486
  175.7 11.1 %collective-permute-start.19 = (f32[112,256]{1,0:T(8,128)S(1)}, f32[112,256]{1,0:T(8,128)S(1)}, u32[]{:S(2)}, u32[]{:S(2)}) collective-permute-start(f32[112,256]{1,0:T(8,128)S(1)} %pad_maximum_fusion.4.rest_0_), channel_id=1, source_target_pairs={{0,64},{32,96},{64,128},{96,160},{128,192},{160,224},{192,0},{224,... | collective-permute-start | bytes 344072 | tf_op jit(solution)/shard_map/sum_and_invert/ppermute | solution.py:486
  186.8 6.3 %copy-start.1 = (f32[256,256]{1,0:T(8,128)}, f32[256,256]{1,0:T(8,128)S(1)}, u32[]{:S(2)}) copy-start(f32[256,256]{1,0:T(8,128)S(1)} %second_inverse.1.inverse_ref) | copy-start | bytes 786436
  188.2 14.7 %all-to-all-start.6 = ((f32[32,1,256]{2,1,0:T(1,128)}), f32[32,1,256]{2,1,0:T(1,128)S(1)}, u32[]{:S(2)}, u32[]{:S(2)}) async-start(f32[32,1,256]{2,1,0:T(1,128)} %get-tuple-element.47), calls=%async_computation.6 | async-start | bytes 65536 | tf_op jit(solution)/shard_map/all_to_all | solution.py:502
  193.1 1.0 copy-start.2
  194.0 1.2 copy-start.4
